TPU v7x, 32 devices: a whole 2x2x4 slice. The times are simulated.
32 devices in a mesh: dp: 4 (over y, core), fsdp: 8 (over z, x).
Axes of the slice: x: 2, y: 2, z: 4, core: 2. Of those that a mesh axis runs over, the one named last changes fastest.
Arguments:
- tokens: bfloat16 [16384, 768], P(('dp', 'fsdp')), may hold values from -8 to 8
- doc_lengths: int32 [32], P(('dp', 'fsdp')), may hold values from 128 to 512, as said below
- w_query: bfloat16 [768, 768], P('dp', 'fsdp'), may hold values from -0.21875 to 0.21875
- w_key: bfloat16 [768, 768], P('dp', 'fsdp'), may hold values from -0.21875 to 0.21875
- w_value: bfloat16 [768, 768], P('dp', 'fsdp'), may hold values from -0.21875 to 0.21875
- w_query2: bfloat16 [768, 768], P('dp', 'fsdp'), may hold values from -1.75 to 1.75
- w_key2: bfloat16 [768, 768], P('dp', 'fsdp'), may hold values from -0.21875 to 0.21875
- w_value2: bfloat16 [768, 768], P('dp', 'fsdp'), may hold values from -0.21875 to 0.21875
- w_out: bfloat16 [768, 768], P('dp', 'fsdp'), may hold values from -1.25 to 1.25
- w_up: bfloat16 [768, 3072], P('dp', 'fsdp'), may hold values from -0.21875 to 0.21875
- w_down: bfloat16 [3072, 768], P('dp', 'fsdp'), may hold values from -0.109375 to 0.109375
- norm_gains: float32 [2, 768], replicated, may hold values from 0.5 to 1.5
- norm_shifts: float32 [2, 768], replicated, may hold values from -3 to 3
- pool_kernels: float32 [2, 5, 768], replicated, may hold values from -2.5 to 2.5
- out_grad: bfloat16 [16384, 768], P(('dp', 'fsdp')), may hold values from -8 to 8
Outputs:
- activations: bfloat16 [16384, 768], P(('dp', 'fsdp'))
- input_grad: bfloat16 [16384, 768], P(('dp', 'fsdp'))
- grad_w_query: float32 [768, 768], P('dp', 'fsdp')
- grad_w_key: float32 [768, 768], P('dp', 'fsdp')
- grad_w_value: float32 [768, 768], P('dp', 'fsdp')
- grad_w_query2: float32 [768, 768], P('dp', 'fsdp')
- grad_w_key2: float32 [768, 768], P('dp', 'fsdp')
- grad_w_value2: float32 [768, 768], P('dp', 'fsdp')
- grad_w_out: float32 [768, 768], P('dp', 'fsdp')
- grad_w_up: float32 [768, 3072], P('dp', 'fsdp')
- grad_w_down: float32 [3072, 768], P('dp', 'fsdp')
- grad_gains: float32 [2, 768], replicated
- grad_shifts: float32 [2, 768], replicated
- grad_pools: float32 [2, 5, 768], replicated
Inputs may be any that keep to these rules, and one draw needn't show every extreme that they name: `doc_lengths`: every entry is a multiple of 128; some entry equals 512.
All inputs are finite; a program needn't handle non-finite values.
Results may differ from a plain program's by a relative error of at most 0.038.
The roundings to bfloat16 on the way count: a program that leaves them out, or rounds other values in their place, can miss the bound.
Values may be sent and summed in bfloat16 or wider, within the bound.
A program may use at most 192 MiB of HBM per device.

v0:
```python
import math

import jax
import jax.numpy as jnp
from jax import lax
from jax.sharding import PartitionSpec as P

HEADS = 12
HD = 64
WIN = 128
PWIN = 512
STRIDE = 4


def matmul(left_mat, right_mat):
    return jnp.dot(left_mat, right_mat, preferred_element_type=jnp.float32)


def inner_rows(left_mat, right_mat):
    return lax.dot_general(
        left_mat, right_mat, (((0,), (0,)), ((), ())), preferred_element_type=jnp.float32
    )


def outer_cols(left_mat, right_mat):
    return lax.dot_general(
        left_mat, right_mat, (((1,), (1,)), ((), ())), preferred_element_type=jnp.float32
    )


def layer_norm(inputs, norm_gain, norm_shift):
    average = jnp.mean(inputs, axis=-1, keepdims=True)
    centred = inputs - average
    variance = jnp.mean(centred * centred, axis=-1, keepdims=True)
    return centred * lax.rsqrt(variance + 1e-05) * norm_gain + norm_shift


def gelu_tanh(inputs):
    return jax.nn.gelu(inputs, approximate=True)


def pool_rows(inputs, kernel):
    side_rows = (kernel.shape[0] - 1) // 2
    pooled_rows = inputs.shape[0] // STRIDE
    padded = jnp.pad(inputs, ((side_rows, side_rows), (0, 0)))
    summed = jnp.zeros((pooled_rows, inputs.shape[1]), jnp.float32)
    for offset in range(kernel.shape[0]):
        summed = summed + kernel[offset] * padded[offset : offset + inputs.shape[0] : STRIDE]
    return summed


def split_heads(matrix):
    return matrix.reshape(matrix.shape[0], HEADS // 2, 2, HD).transpose(1, 0, 2, 3)


def join_heads(groups):
    return groups.transpose(1, 0, 2, 3).reshape(groups.shape[1], HEADS * HD)


def masked_scores(query, keys, allowed, score_scale):
    raw_scores = (
        jnp.einsum("ihd,jhd->hij", query, keys, preferred_element_type=jnp.float32) * score_scale
    )
    return jnp.where(allowed[None], raw_scores, -1e30)


def attend_forward(query, keys, values, allowed, score_scale):
    scores = masked_scores(query, keys, allowed, score_scale)
    highest = jnp.max(scores, axis=-1, keepdims=True)
    expo_terms = jnp.exp(scores - highest)
    summed = jnp.sum(expo_terms, axis=-1, keepdims=True)
    soft_weights = (expo_terms / summed).astype(jnp.bfloat16)
    result = jnp.einsum("hij,jhd->ihd", soft_weights, values, preferred_element_type=jnp.float32)
    return (result, (highest + jnp.log(summed))[..., 0])


def attend_backward(query, keys, values, allowed, score_scale, log_total, grad_result):
    scores = masked_scores(query, keys, allowed, score_scale)
    soft_weights = jnp.exp(scores - log_total[..., None])
    grad_soft = jnp.einsum("ihd,jhd->hij", grad_result, values, preferred_element_type=jnp.float32)
    grad_values = jnp.einsum(
        "hij,ihd->jhd",
        soft_weights.astype(jnp.bfloat16),
        grad_result,
        preferred_element_type=jnp.float32,
    )
    row_terms = jnp.sum(soft_weights * grad_soft, axis=-1, keepdims=True)
    grad_scores = (soft_weights * (grad_soft - row_terms)).astype(jnp.bfloat16)
    grad_query = (
        jnp.einsum("hij,jhd->ihd", grad_scores, keys, preferred_element_type=jnp.float32)
        * score_scale
    )
    grad_keys = (
        jnp.einsum("hij,ihd->jhd", grad_scores, query, preferred_element_type=jnp.float32)
        * score_scale
    )
    return (grad_query, grad_keys, grad_values)


def level_forward(query, keys, values, allowed, score_scale):

    def one_group(group_parts):
        return attend_forward(group_parts[0], group_parts[1], group_parts[2], allowed, score_scale)

    results, log_totals = lax.map(
        one_group, (split_heads(query), split_heads(keys), split_heads(values))
    )
    return (join_heads(results), log_totals)


def level_backward(query, keys, values, allowed, score_scale, log_totals, grad_result):

    def one_group(group_parts):
        return attend_backward(
            group_parts[0],
            group_parts[1],
            group_parts[2],
            allowed,
            score_scale,
            group_parts[3],
            group_parts[4],
        )

    grad_query, grad_keys, grad_values = lax.map(
        one_group,
        (
            split_heads(query),
            split_heads(keys),
            split_heads(values),
            log_totals,
            split_heads(grad_result),
        ),
    )
    return (join_heads(grad_query), join_heads(grad_keys), join_heads(grad_values))


def gather_first(shards):
    column_parts = (
        lax.all_gather(shards[0], "fsdp", axis=1, tiled=True),
        lax.all_gather(shards[1], "fsdp", axis=1, tiled=True),
        lax.all_gather(shards[2], "fsdp", axis=1, tiled=True),
        lax.all_gather(shards[3], "fsdp", axis=1, tiled=True),
        lax.all_gather(shards[4], "fsdp", axis=1, tiled=True),
        lax.all_gather(shards[5], "fsdp", axis=1, tiled=True),
        lax.all_gather(shards[6], "fsdp", axis=1, tiled=True),
        lax.all_gather(shards[7], "fsdp", axis=1, tiled=True),
        lax.all_gather(shards[8], "fsdp", axis=1, tiled=True),
    )
    return (
        lax.all_gather(column_parts[0], "dp", axis=0, tiled=True),
        lax.all_gather(column_parts[1], "dp", axis=0, tiled=True),
        lax.all_gather(column_parts[2], "dp", axis=0, tiled=True),
        lax.all_gather(column_parts[3], "dp", axis=0, tiled=True),
        lax.all_gather(column_parts[4], "dp", axis=0, tiled=True),
        lax.all_gather(column_parts[5], "dp", axis=0, tiled=True),
        lax.all_gather(column_parts[6], "dp", axis=0, tiled=True),
        lax.all_gather(column_parts[7], "dp", axis=0, tiled=True),
        lax.all_gather(column_parts[8], "dp", axis=0, tiled=True),
    )


def gather_second(shards):
    column_parts = (
        lax.all_gather(shards[0], "fsdp", axis=1, tiled=True),
        lax.all_gather(shards[1], "fsdp", axis=1, tiled=True),
        lax.all_gather(shards[2], "fsdp", axis=1, tiled=True),
        lax.all_gather(shards[3], "fsdp", axis=1, tiled=True),
        lax.all_gather(shards[4], "fsdp", axis=1, tiled=True),
        lax.all_gather(shards[5], "fsdp", axis=1, tiled=True),
        lax.all_gather(shards[6], "fsdp", axis=1, tiled=True),
        lax.all_gather(shards[7], "fsdp", axis=1, tiled=True),
        lax.all_gather(shards[8], "fsdp", axis=1, tiled=True),
    )
    return (
        lax.all_gather(column_parts[0], "dp", axis=0, tiled=True),
        lax.all_gather(column_parts[1], "dp", axis=0, tiled=True),
        lax.all_gather(column_parts[2], "dp", axis=0, tiled=True),
        lax.all_gather(column_parts[3], "dp", axis=0, tiled=True),
        lax.all_gather(column_parts[4], "dp", axis=0, tiled=True),
        lax.all_gather(column_parts[5], "dp", axis=0, tiled=True),
        lax.all_gather(column_parts[6], "dp", axis=0, tiled=True),
        lax.all_gather(column_parts[7], "dp", axis=0, tiled=True),
        lax.all_gather(column_parts[8], "dp", axis=0, tiled=True),
    )


def reduce_columns_first(grads_all):
    column_sums = (
        lax.psum_scatter(
            grads_all[0].astype(jnp.bfloat16), "fsdp", scatter_dimension=1, tiled=True
        ).astype(jnp.float32),
        lax.psum_scatter(
            grads_all[1].astype(jnp.bfloat16), "fsdp", scatter_dimension=1, tiled=True
        ).astype(jnp.float32),
        lax.psum_scatter(
            grads_all[2].astype(jnp.bfloat16), "fsdp", scatter_dimension=1, tiled=True
        ).astype(jnp.float32),
        lax.psum_scatter(
            grads_all[3].astype(jnp.bfloat16), "fsdp", scatter_dimension=1, tiled=True
        ).astype(jnp.float32),
        lax.psum_scatter(
            grads_all[4].astype(jnp.bfloat16), "fsdp", scatter_dimension=1, tiled=True
        ).astype(jnp.float32),
        lax.psum_scatter(
            grads_all[5].astype(jnp.bfloat16), "fsdp", scatter_dimension=1, tiled=True
        ).astype(jnp.float32),
        lax.psum_scatter(
            grads_all[6].astype(jnp.bfloat16), "fsdp", scatter_dimension=1, tiled=True
        ).astype(jnp.float32),
        lax.psum_scatter(
            grads_all[7].astype(jnp.bfloat16), "fsdp", scatter_dimension=1, tiled=True
        ).astype(jnp.float32),
        lax.psum_scatter(
            grads_all[8].astype(jnp.bfloat16), "fsdp", scatter_dimension=1, tiled=True
        ).astype(jnp.float32),
    )
    return (
        lax.psum_scatter(
            column_sums[0].astype(jnp.bfloat16), "dp", scatter_dimension=0, tiled=True
        ).astype(jnp.float32),
        lax.psum_scatter(
            column_sums[1].astype(jnp.bfloat16), "dp", scatter_dimension=0, tiled=True
        ).astype(jnp.float32),
        lax.psum_scatter(
            column_sums[2].astype(jnp.bfloat16), "dp", scatter_dimension=0, tiled=True
        ).astype(jnp.float32),
        lax.psum_scatter(
            column_sums[3].astype(jnp.bfloat16), "dp", scatter_dimension=0, tiled=True
        ).astype(jnp.float32),
        lax.psum_scatter(
            column_sums[4].astype(jnp.bfloat16), "dp", scatter_dimension=0, tiled=True
        ).astype(jnp.float32),
        lax.psum_scatter(
            column_sums[5].astype(jnp.bfloat16), "dp", scatter_dimension=0, tiled=True
        ).astype(jnp.float32),
        lax.psum_scatter(
            column_sums[6].astype(jnp.bfloat16), "dp", scatter_dimension=0, tiled=True
        ).astype(jnp.float32),
        lax.psum_scatter(
            column_sums[7].astype(jnp.bfloat16), "dp", scatter_dimension=0, tiled=True
        ).astype(jnp.float32),
        lax.psum_scatter(
            column_sums[8].astype(jnp.bfloat16), "dp", scatter_dimension=0, tiled=True
        ).astype(jnp.float32),
    )


def local(
    tokens,
    doc_lengths,
    w_query,
    w_key,
    w_value,
    w_query2,
    w_key2,
    w_value2,
    w_out,
    w_up,
    w_down,
    norm_gains,
    norm_shifts,
    pool_kernels,
    out_grad,
):
    shards = (w_query, w_key, w_value, w_query2, w_key2, w_value2, w_out, w_up, w_down)
    forward_weights = gather_first(shards)
    (
        full_query,
        full_key,
        full_value,
        full_query2,
        full_key2,
        full_value2,
        full_out,
        full_up,
        full_down,
    ) = forward_weights
    seq_rows = tokens.shape[0]
    length = doc_lengths[0]
    positions = jnp.arange(seq_rows, dtype=jnp.int32)
    padding = positions >= length
    allowed_one = (jnp.abs(positions[:, None] - positions[None, :]) <= WIN) & (
        padding[:, None] == padding[None, :]
    )
    pooled_at = positions[: seq_rows // STRIDE] * STRIDE
    allowed_two = (jnp.abs(positions[:, None] - pooled_at[None, :]) <= PWIN // 2) & (
        padding[:, None] == (pooled_at >= length)[None, :]
    )
    score_scale = 1.0 / math.sqrt(HD)
    query = matmul(tokens, full_query).astype(jnp.bfloat16)
    keys = matmul(tokens, full_key).astype(jnp.bfloat16)
    values = matmul(tokens, full_value).astype(jnp.bfloat16)
    key_two = matmul(tokens, full_key2)
    value_two = matmul(tokens, full_value2)
    key_pool_f, pool_key_back = jax.vjp(pool_rows, key_two, pool_kernels[0])
    value_pool_f, pool_value_back = jax.vjp(pool_rows, value_two, pool_kernels[1])
    key_pool = key_pool_f.astype(jnp.bfloat16)
    value_pool = value_pool_f.astype(jnp.bfloat16)
    first_f, log_one = level_forward(query, keys, values, allowed_one, score_scale)
    first = first_f.astype(jnp.bfloat16)
    query_two = matmul(first, full_query2).astype(jnp.bfloat16)
    second, log_two = level_forward(query_two, key_pool, value_pool, allowed_two, score_scale)
    mixed = (first.astype(jnp.float32) + second).astype(jnp.bfloat16)
    branch = matmul(mixed, full_out)
    hidden, norm_one_back = jax.vjp(
        layer_norm, tokens.astype(jnp.float32) + branch, norm_gains[0], norm_shifts[0]
    )
    hidden_low = hidden.astype(jnp.bfloat16)
    upper = matmul(hidden_low, full_up)
    activated_f, gelu_back = jax.vjp(gelu_tanh, upper)
    activated = activated_f.astype(jnp.bfloat16)
    resid_two = hidden + matmul(activated, full_down)
    result, norm_two_back = jax.vjp(layer_norm, resid_two, norm_gains[1], norm_shifts[1])
    activations = result.astype(jnp.bfloat16)
    back_weights = gather_second(shards)
    (
        back_query,
        back_key,
        back_value,
        back_query2,
        back_key2,
        back_value2,
        back_out,
        back_up,
        back_down,
    ) = back_weights
    d_resid_two, d_gain_two, d_shift_two = norm_two_back(out_grad.astype(jnp.float32))
    d_ffn = d_resid_two.astype(jnp.bfloat16)
    grad_down = inner_rows(activated, d_ffn)
    d_upper = gelu_back(outer_cols(d_ffn, back_down))[0].astype(jnp.bfloat16)
    grad_up = inner_rows(hidden_low, d_upper)
    d_hidden = d_resid_two + outer_cols(d_upper, back_up)
    d_resid_one, d_gain_one, d_shift_one = norm_one_back(d_hidden)
    d_branch = d_resid_one.astype(jnp.bfloat16)
    grad_out = inner_rows(mixed, d_branch)
    d_mixed = outer_cols(d_branch, back_out)
    d_query_two_f, d_key_pool_f, d_value_pool_f = level_backward(
        query_two,
        key_pool,
        value_pool,
        allowed_two,
        score_scale,
        log_two,
        d_mixed.astype(jnp.bfloat16),
    )
    d_query_two = d_query_two_f.astype(jnp.bfloat16)
    d_key_pool = d_key_pool_f.astype(jnp.bfloat16)
    d_value_pool = d_value_pool_f.astype(jnp.bfloat16)
    grad_query2 = inner_rows(first, d_query_two)
    d_first = (d_mixed + outer_cols(d_query_two, back_query2)).astype(jnp.bfloat16)
    d_query_f, d_keys_f, d_values_f = level_backward(
        query, keys, values, allowed_one, score_scale, log_one, d_first
    )
    d_query = d_query_f.astype(jnp.bfloat16)
    d_keys = d_keys_f.astype(jnp.bfloat16)
    d_values = d_values_f.astype(jnp.bfloat16)
    d_key_two_f, d_pool_key = pool_key_back(d_key_pool.astype(jnp.float32))
    d_value_two_f, d_pool_value = pool_value_back(d_value_pool.astype(jnp.float32))
    d_key_two = d_key_two_f.astype(jnp.bfloat16)
    d_value_two = d_value_two_f.astype(jnp.bfloat16)
    grad_query = inner_rows(tokens, d_query)
    grad_key = inner_rows(tokens, d_keys)
    grad_value = inner_rows(tokens, d_values)
    grad_key2 = inner_rows(tokens, d_key_two)
    grad_value2 = inner_rows(tokens, d_value_two)
    d_tokens = (
        d_resid_one
        + outer_cols(d_query, back_query)
        + outer_cols(d_keys, back_key)
        + outer_cols(d_values, back_value)
    )
    d_tokens = d_tokens + outer_cols(d_key_two, back_key2) + outer_cols(d_value_two, back_value2)
    grads_all = (
        grad_query,
        grad_key,
        grad_value,
        grad_query2,
        grad_key2,
        grad_value2,
        grad_out,
        grad_up,
        grad_down,
    )
    owned = reduce_columns_first(grads_all)
    gain_stack = jnp.stack([d_gain_one, d_gain_two])
    shift_stack = jnp.stack([d_shift_one, d_shift_two])
    pool_stack = jnp.stack([d_pool_key, d_pool_value])
    vector_sums = lax.psum((gain_stack, shift_stack, pool_stack), ("dp", "fsdp"))
    return (
        activations,
        d_tokens.astype(jnp.bfloat16),
        owned[0],
        owned[1],
        owned[2],
        owned[3],
        owned[4],
        owned[5],
        owned[6],
        owned[7],
        owned[8],
        vector_sums[0],
        vector_sums[1],
        vector_sums[2],
    )


def solution(mesh):
    return jax.shard_map(
        local,
        mesh=mesh,
        in_specs=(
            P(("dp", "fsdp"), None),
            P(("dp", "fsdp")),
            P("dp", "fsdp"),
            P("dp", "fsdp"),
            P("dp", "fsdp"),
            P("dp", "fsdp"),
            P("dp", "fsdp"),
            P("dp", "fsdp"),
            P("dp", "fsdp"),
            P("dp", "fsdp"),
            P("dp", "fsdp"),
            P(),
            P(),
            P(),
            P(("dp", "fsdp"), None),
        ),
        out_specs=(
            P(("dp", "fsdp"), None),
            P(("dp", "fsdp"), None),
            P("dp", "fsdp"),
            P("dp", "fsdp"),
            P("dp", "fsdp"),
            P("dp", "fsdp"),
            P("dp", "fsdp"),
            P("dp", "fsdp"),
            P("dp", "fsdp"),
            P("dp", "fsdp"),
            P("dp", "fsdp"),
            P(),
            P(),
            P(),
        ),
        check_vma=False,
    )
```

profile of v0, /device:TPU:1, one launch (start us, length us, event | category | flops | bytes accessed | tf_op | source)
XLA Modules:
  0.0 1317.8 jit_solution(14509883090069733292)
XLA Ops:
  8.1 26.2 %all_gather.82 = bf16[192,768]{0,1:T(8,128)(2,1)S(1)} all-gather(bf16[192,96]{0,1:T(8,128)(2,1)S(1)} %copy.172), channel_id=1, replica_groups=mesh['dp'=4,'fsdp'=8] {'fsdp'}, dimensions={1}, use_global_device_ids=true | all-gather | bytes 331776 | tf_op jit(solution)/shard_map/all_gather | solution.py:143
  36.2 24.8 %all_gather.78 = bf16[192,768]{0,1:T(8,128)(2,1)S(1)} all-gather(bf16[192,96]{0,1:T(8,128)(2,1)S(1)} %copy.166), channel_id=1, replica_groups=mesh['dp'=4,'fsdp'=8] {'fsdp'}, dimensions={1}, use_global_device_ids=true | all-gather | bytes 331776 | tf_op jit(solution)/shard_map/all_gather | solution.py:144
  62.1 24.8 %all_gather.72 = bf16[192,768]{0,1:T(8,128)(2,1)S(1)} all-gather(bf16[192,96]{0,1:T(8,128)(2,1)S(1)} %copy.157), channel_id=1, replica_groups=mesh['dp'=4,'fsdp'=8] {'fsdp'}, dimensions={1}, use_global_device_ids=true | all-gather | bytes 331776 | tf_op jit(solution)/shard_map/all_gather | solution.py:141
  87.9 24.7 %all_gather.74 = bf16[192,768]{0,1:T(8,128)(2,1)S(1)} all-gather(bf16[192,96]{0,1:T(8,128)(2,1)S(1)} %copy.160), channel_id=1, replica_groups=mesh['dp'=4,'fsdp'=8] {'fsdp'}, dimensions={1}, use_global_device_ids=true | all-gather | bytes 331776 | tf_op jit(solution)/shard_map/all_gather | solution.py:139
  113.7 24.8 %all_gather.76 = bf16[192,768]{0,1:T(8,128)(2,1)S(1)} all-gather(bf16[192,96]{0,1:T(8,128)(2,1)S(1)} %copy.163), channel_id=1, replica_groups=mesh['dp'=4,'fsdp'=8] {'fsdp'}, dimensions={1}, use_global_device_ids=true | all-gather | bytes 331776 | tf_op jit(solution)/shard_map/all_gather | solution.py:140
  140.2 25.0 %all_gather.80 = bf16[192,768]{0,1:T(8,128)(2,1)S(1)} all-gather(bf16[192,96]{0,1:T(8,128)(2,1)S(1)} %copy.169), channel_id=1, replica_groups=mesh['dp'=4,'fsdp'=8] {'fsdp'}, dimensions={1}, use_global_device_ids=true | all-gather | bytes 331776 | tf_op jit(solution)/shard_map/all_gather | solution.py:142
  167.0 25.1 %all_gather.84 = bf16[192,768]{0,1:T(8,128)(2,1)S(1)} all-gather(bf16[192,96]{0,1:T(8,128)(2,1)S(1)} %copy.175), channel_id=1, replica_groups=mesh['dp'=4,'fsdp'=8] {'fsdp'}, dimensions={1}, use_global_device_ids=true | all-gather | bytes 331776 | tf_op jit(solution)/shard_map/all_gather | solution.py:145
  233.0 22.0 %while.60 = (s32[]{:T(128)}, bf16[6,512,2,64]{1,3,2,0:T(8,128)(2,1)S(1)}, f32[6,2,512]{2,1,0:T(2,128)}, bf16[6,512,2,64]{1,3,2,0:T(8,128)(2,1)}, bf16[6,512,2,64...) while((s32[]{:T(128)}, ...), condition=%wide.region_3.4_spmd.clone.clone, body=%wide.region_0.3_spmd.clone.sunk.clone | while | flops 141818880 | bytes 8031309 | solution.py:105
  260.3 32.7 %all-gather.30.cloned.1.call-done = bf16[768,768]{0,1:T(8,128)(2,1)} async-done(((bf16[768,96]{0,1:T(8,128)(2,1)}), bf16[768,768]{0,1:T(8,128)(2,1)}) %all-gather.30.cloned.1.call-update) | async-done | bytes 1179664 | tf_op jit(solution)/shard_map/all_gather | solution.py:147
  318.7 32.8 %all-gather.28.cloned.1.call-done = bf16[768,3072]{1,0:T(8,128)(2,1)} async-done(((bf16[192,3072]{1,0:T(8,128)(2,1)}), bf16[768,3072]{1,0:T(8,128)(2,1)}) %all-gather.28.cloned.1.call-update) | async-done | bytes 4718608 | tf_op jit(solution)/shard_map/all_gather | solution.py:157
  358.5 32.0 %all-gather.32.cloned.1.call-done = bf16[3072,768]{0,1:T(8,128)(2,1)} async-done(((bf16[768,768]{0,1:T(8,128)(2,1)}), bf16[3072,768]{0,1:T(8,128)(2,1)}) %all-gather.32.cloned.1.call-update) | async-done | bytes 4718608 | tf_op jit(solution)/shard_map/all_gather | solution.py:158
  424.1 44.4 %while.62 = (s32[]{:T(128)}, bf16[6,512,2,64]{1,3,2,0:T(8,128)(2,1)}, bf16[6,128,2,64]{1,3,2,0:T(8,128)(2,1)}, bf16[6,128,2,64]{1,3,2,0:T(8,128)(2,1)}, bf16[6,1...) while((s32[]{:T(128)}, ...), condition=%wide.region_18.19_spmd.clone.clone, body=%wide.region_16.18_spmd.clone.sunk.clone | while | flops 85474304 | bytes 5105913 | solution.py:124
  511.1 54.9 %while.63 = (s32[]{:T(128)}, bf16[6,512,2,64]{1,3,2,0:T(8,128)(2,1)S(1)}, bf16[6,512,2,64]{1,3,2,0:T(8,128)(2,1)}, bf16[6,512,2,64]{1,3,2,0:T(8,128)(2,1)}, bf16...) while((s32[]{:T(128)}, ...), condition=%wide.region_21.22_spmd.clone.clone, body=%wide.region_19.21_spmd.clone.sunk.clone | while | flops 341703680 | bytes 17983080 | solution.py:124
  641.4 64.5 %reduce-scatter.37.cloned.1.call-done = bf16[768,96]{0,1:T(8,128)(2,1)} async-done(((bf16[768,768]{0,1:T(8,128)(2,1)}), bf16[768,96]{0,1:T(8,128)(2,1)}) %reduce-scatter.37.cloned.1.call-update) | async-done | bytes 147472 | tf_op jit(solution)/shard_map/reduce_scatter | solution.py:192
  707.7 64.5 %reduce-scatter.39.cloned.1.call-done = bf16[768,96]{0,1:T(8,128)(2,1)} async-done(((bf16[768,768]{0,1:T(8,128)(2,1)}), bf16[768,96]{0,1:T(8,128)(2,1)}) %reduce-scatter.39.cloned.1.call-update) | async-done | bytes 147472 | tf_op jit(solution)/shard_map/reduce_scatter | solution.py:195
  774.0 64.5 %reduce-scatter.43.cloned.1.call-done = bf16[768,96]{0,1:T(8,128)(2,1)} async-done(((bf16[768,768]{0,1:T(8,128)(2,1)}), bf16[768,96]{0,1:T(8,128)(2,1)}) %reduce-scatter.43.cloned.1.call-update) | async-done | bytes 147472 | tf_op jit(solution)/shard_map/reduce_scatter | solution.py:201
  840.3 64.5 %reduce-scatter.41.cloned.1.call-done = bf16[768,96]{0,1:T(8,128)(2,1)} async-done(((bf16[768,768]{0,1:T(8,128)(2,1)}), bf16[768,96]{0,1:T(8,128)(2,1)}) %reduce-scatter.41.cloned.1.call-update) | async-done | bytes 147472 | tf_op jit(solution)/shard_map/reduce_scatter | solution.py:198
  906.8 97.4 %reduce-scatter.51.cloned.1.call-done = bf16[3072,96]{0,1:T(8,128)(2,1)} async-done(((bf16[3072,768]{0,1:T(8,128)(2,1)}), bf16[3072,96]{0,1:T(8,128)(2,1)}) %reduce-scatter.51.cloned.1.call-update) | async-done | bytes 589840 | tf_op jit(solution)/shard_map/reduce_scatter | solution.py:213
  1004.5 43.2 %all-reduce.22 = (f32[2,768]{1,0:T(2,128)}, f32[2,768]{1,0:T(2,128)}, f32[2,5,768]{2,1,0:T(8,128)S(1)}) all-reduce(f32[2,768]{1,0:T(2,128)S(1)} %pad_maximum_fusion.1, f32[2,768]{1,0:T(2,128)S(1)} %pad_maximum_fusion.2, f32[2,5,768]{2,1,0:T(8,128)S(1)} %pad_maximum_fusion), channel_id=1, replica_groups=mesh['dp'=4,'fsdp'=8] {'dp','fsdp'}, use_global_device_ids=true, to_apply=%region_42.43 | all-reduce | flops 10752 | bytes 86016 | tf_op jit(solution)/shard_map/psum | solution.py:388
  1053.7 50.2 %reduce-scatter.69.cloned.1.call-done = bf16[384,768]{1,0:T(8,128)(2,1)} async-done(((bf16[3072,768]{1,0:T(8,128)(2,1)}), bf16[384,768]{1,0:T(8,128)(2,1)}) %reduce-scatter.69.cloned.1.call-update) | async-done | bytes 589840
  1149.6 21.2 %reduce-scatter.55.cloned.1.call-done = bf16[192,96]{1,0:T(8,128)(2,1)} async-done(((bf16[768,96]{1,0:T(8,128)(2,1)}), bf16[192,96]{1,0:T(8,128)(2,1)}) %reduce-scatter.55.cloned.1.call-update) | async-done | bytes 36880
  1172.4 21.0 %reduce-scatter.57.cloned.1.call-done = bf16[192,96]{1,0:T(8,128)(2,1)} async-done(((bf16[768,96]{1,0:T(8,128)(2,1)}), bf16[192,96]{1,0:T(8,128)(2,1)}) %reduce-scatter.57.cloned.1.call-update) | async-done | bytes 36880
  1261.4 23.1 %reduce-scatter.53.cloned.1.call-done = bf16[768,96]{0,1:T(8,128)(2,1)} async-done(((bf16[3072,96]{0,1:T(8,128)(2,1)}), bf16[768,96]{0,1:T(8,128)(2,1)}) %reduce-scatter.53.cloned.1.call-update) | async-done | bytes 147472 | tf_op jit(solution)/shard_map/reduce_scatter | solution.py:242
  1286.2 23.0 %reduce-scatter.49.cloned.1.call-done = bf16[192,384]{1,0:T(8,128)(2,1)} async-done(((bf16[768,384]{1,0:T(8,128)(2,1)}), bf16[192,384]{1,0:T(8,128)(2,1)}) %reduce-scatter.49.cloned.1.call-update) | async-done | bytes 147472 | tf_op jit(solution)/shard_map/reduce_scatter | solution.py:239
  (582 shorter events, 508.3 us)
Async XLA Ops:
  7.2 191.0 %all-gather.22.cloned.1.call-start = ((), (), s32[]{:S(2)}) async-start(), calls=%async_computation.23 | async-start | bytes 1474560 | tf_op jit(solution)/shard_map/all_gather | solution.py:154
  35.2 171.3 %all-gather.18.cloned.1.call-start = ((), (), s32[]{:S(2)}) async-start(), calls=%async_computation.21 | async-start | bytes 1474560 | tf_op jit(solution)/shard_map/all_gather | solution.py:155
  61.9 159.6 %all-gather.12.cloned.1.call-start = ((), (), s32[]{:S(2)}) async-start(), calls=%async_computation.18 | async-start | bytes 1474560 | tf_op jit(solution)/shard_map/all_gather | solution.py:152
  87.7 137.3 %all-gather.14.cloned.1.call-start = ((), (), s32[]{:S(2)}) async-start(), calls=%async_computation.19 | async-start | bytes 1474560 | tf_op jit(solution)/shard_map/all_gather | solution.py:150
  166.8 147.1 %all-gather.24.cloned.1.call-start = ((), (), s32[]{:S(2)}) async-start(), calls=%async_computation.24 | async-start | bytes 1474560 | tf_op jit(solution)/shard_map/all_gather | solution.py:156
  193.0 158.5 %all-gather.28.cloned.1.call-start = ((), (), s32[]{:S(2)}) async-start(), calls=%async_computation.26 | async-start | bytes 5898240 | tf_op jit(solution)/shard_map/all_gather | solution.py:157
  231.9 158.7 %all-gather.32.cloned.1.call-start = ((), (), s32[]{:S(2)}) async-start(), calls=%async_computation.28 | async-start | bytes 5898240 | tf_op jit(solution)/shard_map/all_gather | solution.py:158
  293.0 340.4 %reduce-scatter.47.cloned.1.call-start = ((), (), s32[]{:S(2)}) async-start(), calls=%async_computation.35 | async-start | bytes 1327104 | tf_op jit(solution)/shard_map/reduce_scatter | solution.py:207
  424.0 211.3 %reduce-scatter.45.cloned.1.call-start = ((), (), s32[]{:S(2)}) async-start(), calls=%async_computation.34 | async-start | bytes 1327104 | tf_op jit(solution)/shard_map/reduce_scatter | solution.py:204
  569.0 136.9 %reduce-scatter.37.cloned.1.call-start = ((), (), s32[]{:S(2)}) async-start(), calls=%async_computation.30 | async-start | bytes 1327104 | tf_op jit(solution)/shard_map/reduce_scatter | solution.py:192
  572.1 200.2 %reduce-scatter.39.cloned.1.call-start = ((), (), s32[]{:S(2)}) async-start(), calls=%async_computation.31 | async-start | bytes 1327104 | tf_op jit(solution)/shard_map/reduce_scatter | solution.py:195
  575.4 263.1 %reduce-scatter.43.cloned.1.call-start = ((), (), s32[]{:S(2)}) async-start(), calls=%async_computation.33 | async-start | bytes 1327104 | tf_op jit(solution)/shard_map/reduce_scatter | solution.py:201
  606.9 297.8 %reduce-scatter.41.cloned.1.call-start = ((), (), s32[]{:S(2)}) async-start(), calls=%async_computation.32 | async-start | bytes 1327104 | tf_op jit(solution)/shard_map/reduce_scatter | solution.py:198
  610.0 394.3 %reduce-scatter.51.cloned.1.call-start = ((), (), s32[]{:S(2)}) async-start(), calls=%async_computation.37 | async-start | bytes 5308416 | tf_op jit(solution)/shard_map/reduce_scatter | solution.py:213
  618.6 485.3 %reduce-scatter.69.cloned.1.call-start = ((), (), s32[]{:S(2)}) async-start(), calls=%async_computation.46 | async-start | bytes 5308416
  633.3 492.4 %reduce-scatter.67.cloned.1.call-start = ((), (), s32[]{:S(2)}) async-start(), calls=%async_computation.45 | async-start | bytes 245760
  635.2 512.7 %reduce-scatter.65.cloned.1.call-start = ((), (), s32[]{:S(2)}) async-start(), calls=%async_computation.44 | async-start | bytes 245760
  637.1 533.6 %reduce-scatter.55.cloned.1.call-start = ((), (), s32[]{:S(2)}) async-start(), calls=%async_computation.39 | async-start | bytes 245760
  641.3 552.1 %reduce-scatter.57.cloned.1.call-start = ((), (), s32[]{:S(2)}) async-start(), calls=%async_computation.40 | async-start | bytes 245760
  707.7 508.0 %reduce-scatter.59.cloned.1.call-start = ((), (), s32[]{:S(2)}) async-start(), calls=%async_computation.41 | async-start | bytes 245760
  773.9 463.8 %reduce-scatter.63.cloned.1.call-start = ((), (), s32[]{:S(2)}) async-start(), calls=%async_computation.43 | async-start | bytes 245760
  840.2 419.5 %reduce-scatter.61.cloned.1.call-start = ((), (), s32[]{:S(2)}) async-start(), calls=%async_computation.42 | async-start | bytes 245760
  906.5 378.0 %reduce-scatter.53.cloned.1.call-start = ((), (), s32[]{:S(2)}) async-start(), calls=%async_computation.38 | async-start | bytes 737280 | tf_op jit(solution)/shard_map/reduce_scatter | solution.py:242
  1004.3 304.8 %reduce-scatter.49.cloned.1.call-start = ((), (), s32[]{:S(2)}) async-start(), calls=%async_computation.36 | async-start | bytes 737280 | tf_op jit(solution)/shard_map/reduce_scatter | solution.py:239
  (102 other events, 5242.9 us)
Sparse Core Ops, SparseCore 0:
  35.3 24.8 all-gather.21
  62.3 30.6 all-gather.17
  95.2 29.8 all-gather.11
  127.1 30.2 all-gather.13
  158.8 30.9 all-gather.15
  191.6 39.1 all-gather.25
  253.6 39.3 all-gather.29
  313.9 37.4 all-gather.27
  353.0 37.4 all-gather.31
  424.2 62.1 reduce-scatter.46
  511.1 62.0 reduce-scatter.44
  576.5 63.0 reduce-scatter.34
  642.8 63.0 reduce-scatter.36
  709.2 62.9 reduce-scatter.38
  775.4 62.9 reduce-scatter.42
  841.7 62.9 reduce-scatter.40
  908.4 95.8 reduce-scatter.50
  1007.8 96.0 reduce-scatter.68
  1128.2 19.7 reduce-scatter.64
  1151.0 19.7 reduce-scatter.54
  1173.6 19.7 reduce-scatter.56
  1240.0 19.7 reduce-scatter.60
  1262.3 22.2 reduce-scatter.52
  1287.0 22.0 reduce-scatter.48
  (5 shorter events, 95.4 us)
where the time goes:
time: 1330 us; the launch traced here: 1320 us
  waiting for transfers between devices  691 us (52%)
  blocking collectives  219 us (16%)
  matrix products  209 us (16%)
  local copies, waits for them, and re-layouts  131 us (10%)
  other arithmetic  48.3 us (4%)
  between operations  16.8 us (1%)
    unnamed x37, waiting for transfers between devices  190 us
    reduce_scatter x1, waiting for transfers between devices, reduce_columns_first(): lax.psum_scatter(grads_all[8].astype(jnp.bfloat16), 'fsdp', scatter_dimen...  97.4 us
    reduce_scatter x1, waiting for transfers between devices, reduce_columns_first(): lax.psum_scatter(grads_all[1].astype(jnp.bfloat16), 'fsdp', scatter_dimen...  64.5 us
    reduce_scatter x1, waiting for transfers between devices, reduce_columns_first(): lax.psum_scatter(grads_all[4].astype(jnp.bfloat16), 'fsdp', scatter_dimen...  64.5 us
    reduce_scatter x1, waiting for transfers between devices, reduce_columns_first(): lax.psum_scatter(grads_all[2].astype(jnp.bfloat16), 'fsdp', scatter_dimen...  64.5 us
    reduce_scatter x1, waiting for transfers between devices, reduce_columns_first(): lax.psum_scatter(grads_all[3].astype(jnp.bfloat16), 'fsdp', scatter_dimen...  64.5 us
    unnamed x233, local copies, waits for them, and re-layouts  63.8 us
    psum x1, blocking collectives, local(): lax.psum((gain_stack, shift_stack, pool_stack), ('dp', 'fsdp'))  43.2 us
  transfers between devices with their start and end apart: 29, of which 19 were waited for; matrix products, arithmetic and copies ran while one was open for 26% of the time, Pallas kernels for 0%

commit v1 on v0

--- a/solution.py
+++ b/solution.py
@@ -3,6 +3,8 @@
 import jax
 import jax.numpy as jnp
 from jax import lax
+from jax.experimental import pallas as pl
+from jax.experimental.pallas import tpu as pltpu
 from jax.sharding import PartitionSpec as P
 
 HEADS = 12
@@ -242,6 +244,851 @@
         lax.psum_scatter(
             column_sums[8].astype(jnp.bfloat16), "dp", scatter_dimension=0, tiled=True
         ).astype(jnp.float32),
+    )
+
+
+MESH = pl.DeviceIdType.MESH
+BF = jnp.bfloat16
+F32 = jnp.float32
+SQUARE = ((0, 3), (3, 5), (5, 7))
+GROUPS = (0, 1, 2, 3, 4)
+
+
+class Place:
+    def __init__(self):
+        dp = lax.axis_index("dp")
+        fs = lax.axis_index("fsdp")
+        self.y = lax.div(dp, 2)
+        self.c = lax.rem(dp, 2)
+        self.z = lax.div(fs, 2)
+        self.x = lax.rem(fs, 2)
+        c, x, y = self.c, self.x, self.y
+        self.p1 = ((1 - c) * (1 - x) + c * x, (1 - c) * y + c * (1 - y))
+        self.p2 = ((1 - c) * x + c * (1 - x), (1 - c) * (1 - y) + c * y)
+        self.own = (x, y)
+        self.diag = (1 - x, 1 - y)
+
+    def dev(self, xy, z=None, c=None):
+        z = self.z if z is None else z
+        c = self.c if c is None else c
+        return (xy[1] * 2 + c, z * 2 + xy[0])
+
+    def peer(self, k):
+        return lax.rem(self.z + k, 4)
+
+    def everyone(self):
+        return [
+            self.dev(self.own, c=1 - self.c),
+            self.dev(self.p1),
+            self.dev(self.p2),
+            self.dev(self.own, z=self.peer(1)),
+            self.dev(self.own, z=self.peer(2)),
+            self.dev(self.own, z=self.peer(3)),
+        ]
+
+
+def greet(me):
+    bar = pltpu.get_barrier_semaphore()
+    for d in me.everyone():
+        pl.semaphore_signal(bar, inc=1, device_id=d, device_id_type=MESH)
+    pl.semaphore_wait(bar, 6)
+
+
+def quad(refs, g, xy, c, z=None):
+    sq, up, down = refs
+    x, y = xy
+    zz = slice(None) if z is None else z
+    if g < 3:
+        lo, hi = SQUARE[g]
+        return sq.at[lo:hi, zz, x, c, :, pl.ds(pl.multiple_of(y * 384, 128), 384)]
+    if g == 3:
+        return up.at[y, c, zz, x]
+    return down.at[zz, x, :, pl.ds(pl.multiple_of((y * 2 + c) * 768, 128), 768)]
+
+
+def rcopy(src, dst, ssem, rsem, dev):
+    return pltpu.make_async_remote_copy(
+        src_ref=src, dst_ref=dst, send_sem=ssem, recv_sem=rsem, device_id=dev, device_id_type=MESH
+    )
+
+
+class Gather:
+    def __init__(self, me, refs, ssem, rsem):
+        self.me, self.refs, self.ssem, self.rsem = me, refs, ssem, rsem
+
+    def zcopy(self, g, k, incoming):
+        me = self.me
+        z = lax.rem(me.z + 4 - k, 4) if incoming else me.z
+        b = quad(self.refs, g, me.own, me.c, z)
+        return rcopy(b, b, self.ssem.at[g, k - 1], self.rsem.at[g, k - 1], me.dev(me.own, z=me.peer(k)))
+
+    def qcopy(self, g, i, incoming):
+        me = self.me
+        what = {3: (me.own, me.p1), 4: (me.own, me.p2), 5: (me.p1, me.diag)}[i][1 if incoming else 0]
+        b = quad(self.refs, g, what, me.c)
+        return rcopy(b, b, self.ssem.at[g, i], self.rsem.at[g, i], me.dev(me.p1 if i == 3 else me.p2))
+
+    def scopy(self, g, i, incoming):
+        me = self.me
+        what = {
+            6: (me.own, me.own),
+            7: (me.p1, me.p2),
+            8: (me.p2, me.p1),
+            9: (me.diag, me.diag),
+        }[i][1 if incoming else 0]
+        b = quad(self.refs, g, what, (1 - me.c) if incoming else me.c)
+        return rcopy(b, b, self.ssem.at[g, i], self.rsem.at[g, i], me.dev(me.own, c=1 - me.c))
+
+    def start(self, g):
+        for k in (1, 2, 3):
+            self.zcopy(g, k, False).start()
+
+    def step1(self, g):
+        for k in (1, 2, 3):
+            self.zcopy(g, k, True).wait_recv()
+        self.qcopy(g, 3, False).start()
+        self.qcopy(g, 4, False).start()
+        self.scopy(g, 6, False).start()
+
+    def step2(self, g):
+        self.qcopy(g, 3, True).wait_recv()
+        self.qcopy(g, 5, False).start()
+        self.scopy(g, 7, False).start()
+
+    def step3(self, g):
+        self.qcopy(g, 4, True).wait_recv()
+        self.scopy(g, 8, False).start()
+
+    def step4(self, g):
+        self.qcopy(g, 5, True).wait_recv()
+        self.scopy(g, 9, False).start()
+
+    def arrived(self, g):
+        for i in (6, 7, 8, 9):
+            self.scopy(g, i, True).wait_recv()
+
+    def sent(self, g):
+        for k in (1, 2, 3):
+            self.zcopy(g, k, False).wait_send()
+        for i in (3, 4, 5):
+            self.qcopy(g, i, False).wait_send()
+        for i in (6, 7, 8, 9):
+            self.scopy(g, i, False).wait_send()
+
+
+def place_own(me, shards, sq, up, down, contrib, sib, ssem, rsem):
+    rows = lax.broadcasted_iota(jnp.int32, (192, 384), 0)
+    lanes = lax.broadcasted_iota(jnp.int32, (192, 384), 1)
+    spot = jnp.where(lanes == rows + me.c * 192, 1.0, 0.0).astype(BF)
+    for m in range(7):
+        t = lax.dot_general(shards[m][...], spot, (((0,), (0,)), ((), ())), preferred_element_type=F32)
+        t = t.astype(BF)
+        contrib[m, 0] = t[:48]
+        contrib[m, 1] = t[48:]
+    swap = rcopy(contrib.at[:, 1 - me.c], sib, ssem.at[0], rsem.at[0], me.dev(me.own, c=1 - me.c))
+    swap.start()
+    up[me.y, me.c, me.z, me.x] = shards[7][...]
+    eye_r = lax.broadcasted_iota(jnp.int32, (96, 96), 0)
+    eye_c = lax.broadcasted_iota(jnp.int32, (96, 96), 1)
+    eye = jnp.where(eye_r == eye_c, 1.0, 0.0).astype(BF)
+    t = lax.dot_general(eye, shards[8][...], (((1,), (1,)), ((), ())), preferred_element_type=F32)
+    down[me.z, me.x, :, pl.ds(pl.multiple_of((me.y * 2 + me.c) * 768, 128), 768)] = t.astype(BF)
+    swap.wait()
+    for m in range(7):
+        both = contrib[m, me.c].astype(F32) + sib[m].astype(F32)
+        sq[m, me.z, me.x, me.c, :, pl.ds(pl.multiple_of(me.y * 384, 128), 384)] = both.astype(BF)
+
+
+class Scatter:
+    def __init__(self, me, refs, sib, r1, r2, r3, ssem, rsem):
+        self.me, self.refs, self.sib = me, refs, sib
+        self.r1, self.r2, self.r3 = r1, r2, r3
+        self.ssem, self.rsem = ssem, rsem
+
+    def sib_view(self, g, xy, z=None):
+        sq, up, down = self.sib
+        x, y = xy
+        zz = slice(None) if z is None else z
+        if g < 3:
+            lo, hi = SQUARE[g]
+            return sq.at[lo:hi, zz, x, :, pl.ds(pl.multiple_of(y * 384, 128), 384)]
+        if g == 3:
+            return up.at[y, zz, x]
+        return down.at[zz, x, :, pl.ds(pl.multiple_of(y * 768, 128), 768)]
+
+    def slot(self, bufs, g, i):
+        sq, up, down = bufs
+        if g < 3:
+            lo, hi = SQUARE[g]
+            return sq.at[i, lo:hi]
+        return (up if g == 3 else down).at[i]
+
+    def copy(self, g, i):
+        me = self.me
+        ss, rs = self.ssem.at[g, i], self.rsem.at[g, i]
+        if i < 4:
+            what = (me.p1, me.diag, me.p2, me.own)[i]
+            return rcopy(
+                quad(self.refs, g, what, 1 - me.c), self.sib_view(g, what), ss, rs, me.dev(me.own, c=1 - me.c)
+            )
+        if i < 6:
+            what = (me.diag, me.p2)[i - 4]
+            return rcopy(quad(self.refs, g, what, me.c), self.slot(self.r1, g, i - 4), ss, rs, me.dev(me.p2))
+        if i == 6:
+            return rcopy(quad(self.refs, g, me.p1, me.c), self.slot(self.r2, g, 0), ss, rs, me.dev(me.p1))
+        k = i - 6
+        return rcopy(
+            quad(self.refs, g, me.own, me.c, me.peer(k)),
+            self.slot(self.r3, g, k - 1),
+            ss,
+            rs,
+            me.dev(me.own, z=me.peer(k)),
+        )
+
+    def add(self, g, xy, other):
+        here = quad(self.refs, g, xy, self.me.c)
+        here[...] = (here[...].astype(F32) + other[...].astype(F32)).astype(BF)
+
+    def start(self, g):
+        for i in range(4):
+            self.copy(g, i).start()
+
+    def step1(self, g):
+        me = self.me
+        for i, what in ((1, me.diag), (0, me.p2)):
+            self.copy(g, i).wait_recv()
+            self.add(g, what, self.sib_view(g, what))
+            self.copy(g, 4 if i == 1 else 5).start()
+
+    def step2(self, g):
+        me = self.me
+        self.copy(g, 2).wait_recv()
+        self.add(g, me.p1, self.sib_view(g, me.p1))
+        self.copy(g, 4).wait_recv()
+        self.add(g, me.p1, self.slot(self.r1, g, 0))
+        self.copy(g, 6).start()
+
+    def step3(self, g):
+        me = self.me
+        self.copy(g, 3).wait_recv()
+        self.add(g, me.own, self.sib_view(g, me.own))
+        self.copy(g, 5).wait_recv()
+        self.add(g, me.own, self.slot(self.r1, g, 1))
+        self.copy(g, 6).wait_recv()
+        self.add(g, me.own, self.slot(self.r2, g, 0))
+        for k in (1, 2, 3):
+            self.copy(g, 6 + k).start()
+
+    def finish(self, g):
+        me = self.me
+        total = quad(self.refs, g, me.own, me.c, me.z)[...].astype(F32)
+        for k in (1, 2, 3):
+            self.copy(g, 6 + k).wait_recv()
+            total = total + self.slot(self.r3, g, k - 1)[...].astype(F32)
+        return total
+
+    def sent(self, g):
+        for i in range(10):
+            self.copy(g, i).wait_send()
+
+
+GAIN, SHIFT, POOL = 0, 2, 4
+
+
+def dg(a, b, ca, cb):
+    return lax.dot_general(a, b, (((ca,), (cb,)), ((), ())), preferred_element_type=F32)
+
+
+def weight(r, m):
+    return r.sq[m].reshape(768, 768)
+
+
+def weight_up(r, j):
+    left = r.up[:, :, j, 0].reshape(768, 384)
+    right = r.up[:, :, j, 1].reshape(768, 384)
+    return jnp.concatenate([left, right], axis=1)
+
+
+def down_lanes(j):
+    return pl.ds(pl.multiple_of(j * 768, 128), 768)
+
+
+def weight_down(r, j):
+    return r.down[:, :, :, down_lanes(j)].reshape(768, 768)
+
+
+def set_masks(r, length):
+    for i in range(2):
+        row = lax.broadcasted_iota(jnp.int32, (256, 384), 0) + 256 * i
+        col = lax.broadcasted_iota(jnp.int32, (256, 384), 1) + 128 * i
+        ok = (jnp.abs(row - col) <= WIN) & ((row >= length) == (col >= length))
+        r.bias1[i] = jnp.where(ok, 0.0, -1e30)
+    row = lax.broadcasted_iota(jnp.int32, (512, 128), 0)
+    col = lax.broadcasted_iota(jnp.int32, (512, 128), 1) * STRIDE
+    ok = (jnp.abs(row - col) <= PWIN // 2) & ((row >= length) == (col >= length))
+    r.bias2[...] = jnp.where(ok, 0.0, -1e30)
+
+
+def low_lanes(rows):
+    return lax.broadcasted_iota(jnp.int32, (rows, 128), 1) < HD
+
+
+def two_heads(pair):
+    low = low_lanes(pair.shape[0])
+    zero = jnp.zeros_like(pair)
+    return jnp.concatenate([jnp.where(low, pair, zero), jnp.where(low, zero, pair)], axis=0)
+
+
+def side_by_side(stacked):
+    n = stacked.shape[0] // 2
+    return jnp.where(low_lanes(n), stacked[:n], stacked[n:])
+
+
+def pair_lanes(p):
+    return pl.ds(pl.multiple_of(p * 128, 128), 128)
+
+
+def softmax_out(scores, bias, values, lse_ref, p):
+    scores = scores + jnp.concatenate([bias, bias], axis=0)
+    highest = jnp.max(scores, axis=-1, keepdims=True)
+    terms = jnp.exp(scores - highest)
+    summed = jnp.sum(terms, axis=-1, keepdims=True)
+    probs = (terms * (1.0 / summed)).astype(BF)
+    lane = lax.broadcasted_iota(jnp.int32, lse_ref.shape, 1)
+    lse_ref[...] = jnp.where(lane == p, highest + jnp.log(summed), lse_ref[...])
+    return side_by_side(dg(probs, values, 1, 0))
+
+
+def scores_of(query, keys):
+    scaled = two_heads(query * jnp.asarray(0.125, BF))
+    return scaled, dg(scaled, keys, 1, 1)
+
+
+def softmax_back(scores, bias, lse_ref, p, grad, values):
+    scores = scores + jnp.concatenate([bias, bias], axis=0)
+    lane = lax.broadcasted_iota(jnp.int32, lse_ref.shape, 1)
+    lse = jnp.sum(jnp.where(lane == p, lse_ref[...], 0.0), axis=-1, keepdims=True)
+    probs = jnp.exp(scores - lse)
+    grad_probs = dg(grad, values, 1, 1)
+    row_terms = jnp.sum(probs * grad_probs, axis=-1, keepdims=True)
+    return probs.astype(BF), (probs * (grad_probs - row_terms)).astype(BF)
+
+
+def project(r, m):
+    r.qkv[m] = dg(r.tokens[...], weight(r, m), 1, 1).astype(BF)
+
+
+def project_pool(r, i):
+    full = dg(r.tokens[...], weight(r, 3 + i), 1, 1)
+    for l in range(6):
+        lanes = slice(l * 128, l * 128 + 128)
+        r.kt[i, l, 0:8] = jnp.zeros((8, 128), F32)
+        r.kt[i, l, 520:528] = jnp.zeros((8, 128), F32)
+        r.kt[i, l, 8:520] = full[:, lanes]
+        total = None
+        for t in range(5):
+            term = r.pool[i, t : t + 1, lanes] * r.kt[i, l, pl.ds(6 + t, 128, stride=STRIDE), :]
+            total = term if total is None else total + term
+        r.kp[i, :, lanes] = total.astype(BF)
+
+
+def level_one(r):
+    @pl.loop(0, HEADS // 2)
+    def _(p):
+        lanes = pair_lanes(p)
+        for i in range(2):
+            rows, cols = pl.ds(256 * i, 256), pl.ds(128 * i, 384)
+            _, scores = scores_of(r.qkv[0, rows, lanes], r.qkv[1, cols, lanes])
+            out = softmax_out(scores, r.bias1[i], r.qkv[2, cols, lanes], r.lse1.at[i], p)
+            r.first[rows, lanes] = out.astype(BF)
+
+
+def level_two(r):
+    r.q2[...] = dg(r.first[...], weight(r, 5), 1, 1).astype(BF)
+
+    @pl.loop(0, HEADS // 2)
+    def _(p):
+        lanes = pair_lanes(p)
+        _, scores = scores_of(r.q2[:, lanes], r.kp[0, :, lanes])
+        out = softmax_out(scores, r.bias2[...], r.kp[1, :, lanes], r.lse2, p)
+        r.mixed[:, lanes] = (r.first[:, lanes].astype(F32) + out).astype(BF)
+
+
+def norm_parts(x):
+    average = jnp.mean(x, axis=-1, keepdims=True)
+    centred = x - average
+    inverse = lax.rsqrt(jnp.mean(centred * centred, axis=-1, keepdims=True) + 1e-05)
+    return centred * inverse, inverse
+
+
+def norm_back(n, inverse, gain, grad):
+    scaled = grad * gain
+    return (
+        scaled - jnp.mean(scaled, axis=-1, keepdims=True) - n * jnp.mean(scaled * n, axis=-1, keepdims=True)
+    ) * inverse
+
+
+def first_norm(r):
+    r.acc[...] = dg(r.mixed[...], weight(r, 6), 1, 1)
+
+    @pl.loop(0, 4)
+    def _(i):
+        rows = pl.ds(pl.multiple_of(i * 128, 128), 128)
+        n, inverse = norm_parts(r.tokens[rows].astype(F32) + r.acc[rows])
+        r.n1[rows] = n
+        r.inv1[rows] = inverse
+        r.hlow[rows] = (n * r.gains[0:1] + r.shifts[0:1]).astype(BF)
+
+
+def ffn_up(r, j):
+    u = dg(r.hlow[...], weight_up(r, j), 1, 0)
+    k = math.sqrt(2.0 / math.pi)
+    square = u * u
+    t = jnp.tanh(k * u * (1.0 + 0.044715 * square))
+    half = 0.5 * (1.0 + t)
+    r.act[j] = (u * half).astype(BF)
+    slope = half + (0.5 * k) * u * (1.0 - t * t) * (1.0 + (3 * 0.044715) * square)
+    r.gd[j] = slope.astype(BF)
+
+
+def ffn_down_norm(r):
+    for i in range(2):
+        rows = pl.ds(256 * i, 256)
+        total = dg(r.act[0, rows], weight_down(r, 0), 1, 1)
+        for j in range(1, 4):
+            total = total + dg(r.act[j, rows], weight_down(r, j), 1, 1)
+        r.acc[rows] = total
+
+    r.vec[...] = jnp.zeros_like(r.vec)
+
+    @pl.loop(0, 4)
+    def _(i):
+        rows = pl.ds(pl.multiple_of(i * 128, 128), 128)
+        hidden = r.n1[rows] * r.gains[0:1] + r.shifts[0:1]
+        n, inverse = norm_parts(hidden + r.acc[rows])
+        r.out[rows] = (n * r.gains[1:2] + r.shifts[1:2]).astype(BF)
+        grad = r.og[rows].astype(F32)
+        r.vec[GAIN + 1 : GAIN + 2] += jnp.sum(grad * n, axis=0, keepdims=True)
+        r.vec[SHIFT + 1 : SHIFT + 2] += jnp.sum(grad, axis=0, keepdims=True)
+        d = norm_back(n, inverse, r.gains[1:2], grad)
+        r.dr[rows] = d
+        r.dlow[rows] = d.astype(BF)
+
+
+def back_upper(r, j):
+    t = dg(r.dlow[...], weight_down(r, j), 1, 0)
+    r.gd[j] = (r.gd[j].astype(F32) * t).astype(BF)
+
+
+def grad_down(r, j):
+    g = dg(r.dlow[...], r.act[j], 0, 0).astype(BF)
+    r.down[:, :, :, down_lanes(j)] = g.reshape(4, 2, 96, 768)
+
+
+def back_first_norm(r):
+    for i in range(2):
+        rows = pl.ds(256 * i, 256)
+        total = r.dr[rows]
+        for j in range(4):
+            total = total + dg(r.gd[j, rows], weight_up(r, j), 1, 1)
+        r.acc[rows] = total
+
+    @pl.loop(0, 4)
+    def _(i):
+        rows = pl.ds(pl.multiple_of(i * 128, 128), 128)
+        grad = r.acc[rows]
+        n = r.n1[rows]
+        r.vec[GAIN : GAIN + 1] += jnp.sum(grad * n, axis=0, keepdims=True)
+        r.vec[SHIFT : SHIFT + 1] += jnp.sum(grad, axis=0, keepdims=True)
+        d = norm_back(n, r.inv1[rows], r.gains[0:1], grad)
+        r.dr[rows] = d
+        r.dlow[rows] = d.astype(BF)
+
+
+def grad_up(r, j):
+    g = dg(r.hlow[...], r.gd[j], 0, 0).astype(BF)
+    for x in range(2):
+        r.up[:, :, j, x] = g[:, x * 384 : (x + 1) * 384].reshape(2, 2, 192, 384)
+
+
+def set_grad(r, m, left, right):
+    r.sq[m] = dg(left, right, 0, 0).astype(BF).reshape(4, 2, 2, 48, 768)
+
+
+def back_out(r):
+    r.acc[...] = dg(r.dlow[...], weight(r, 6), 1, 0)
+    set_grad(r, 6, r.dlow[...], r.mixed[...])
+
+
+def back_level_two(r):
+    @pl.loop(0, HEADS // 2)
+    def _(p):
+        lanes = pair_lanes(p)
+        scaled, scores = scores_of(r.q2[:, lanes], r.kp[0, :, lanes])
+        grad = two_heads(r.acc[:, lanes].astype(BF))
+        probs, grad_scores = softmax_back(scores, r.bias2[...], r.lse2, p, grad, r.kp[1, :, lanes])
+        r.dpool[1, 0:128, lanes] = dg(probs, grad, 0, 0).astype(BF).astype(F32)
+        r.dpool[0, 0:128, lanes] = dg(grad_scores, scaled, 0, 0).astype(BF).astype(F32)
+        r.dq2[:, lanes] = (side_by_side(dg(grad_scores, r.kp[0, :, lanes], 1, 0)) * 0.125).astype(BF)
+
+    r.dfirst[...] = (r.acc[...] + dg(r.dq2[...], weight(r, 5), 1, 0)).astype(BF)
+    set_grad(r, 5, r.dq2[...], r.first[...])
+
+
+def back_pool(r, i):
+    r.dpool[i, 128:136] = jnp.zeros((8, 768), F32)
+    for l in range(6):
+        lanes = slice(l * 128, l * 128 + 128)
+        here = r.dpool[i, 0:128, lanes]
+        after = r.dpool[i, 1:129, lanes]
+        for t in range(5):
+            term = here * r.kt[i, l, pl.ds(6 + t, 128, stride=STRIDE), :]
+            at = POOL + 5 * i + t
+            r.vec[at : at + 1, lanes] = jnp.sum(term, axis=0, keepdims=True)
+        k = [r.pool[i, t : t + 1, lanes] for t in range(5)]
+        r.kt[i, l, pl.ds(8, 128, stride=STRIDE), :] = k[2] * here
+        r.kt[i, l, pl.ds(9, 128, stride=STRIDE), :] = k[3] * here
+        r.kt[i, l, pl.ds(10, 128, stride=STRIDE), :] = k[4] * here + k[0] * after
+        r.kt[i, l, pl.ds(11, 128, stride=STRIDE), :] = k[1] * after
+    grad = jnp.concatenate([r.kt[i, l, 8:520].astype(BF) for l in range(6)], axis=1)
+    finish_projection(r, 3 + i, grad)
+
+
+def finish_projection(r, m, grad):
+    r.dr[...] = r.dr[...] + dg(grad, weight(r, m), 1, 0)
+    set_grad(r, m, grad, r.tokens[...])
+
+
+def back_level_one(r):
+    @pl.loop(0, HEADS // 2)
+    def _(p):
+        lanes = pair_lanes(p)
+        keys, vals = [], []
+        for i in range(2):
+            rows, cols = pl.ds(256 * i, 256), pl.ds(128 * i, 384)
+            scaled, scores = scores_of(r.qkv[0, rows, lanes], r.qkv[1, cols, lanes])
+            grad = two_heads(r.dfirst[rows, lanes])
+            probs, grad_scores = softmax_back(
+                scores, r.bias1[i], r.lse1.at[i], p, grad, r.qkv[2, cols, lanes]
+            )
+            vals.append(dg(probs, grad, 0, 0))
+            keys.append(dg(grad_scores, scaled, 0, 0))
+            dq = side_by_side(dg(grad_scores, r.qkv[1, cols, lanes], 1, 0)) * 0.125
+            r.dqkv[0, rows, lanes] = dq.astype(BF)
+        for at, parts in ((1, keys), (2, vals)):
+            r.dqkv[at, 0:128, lanes] = parts[0][:128].astype(BF)
+            r.dqkv[at, 128:384, lanes] = (parts[0][128:] + parts[1][:256]).astype(BF)
+            r.dqkv[at, 384:512, lanes] = parts[1][256:].astype(BF)
+
+
+class Refs:
+    pass
+
+
+ACTIVE = dict(
+    qkv=((3, 512, 768), BF),
+    kt=((2, 6, 528, 128), F32),
+    kp=((2, 128, 768), BF),
+    dpool=((2, 136, 768), F32),
+    first=((512, 768), BF),
+    q2=((512, 768), BF),
+    mixed=((512, 768), BF),
+    n1=((512, 768), F32),
+    inv1=((512, 1), F32),
+    hlow=((512, 768), BF),
+    act=((4, 512, 768), BF),
+    gd=((4, 512, 768), BF),
+    dr=((512, 768), F32),
+    acc=((512, 768), F32),
+    dlow=((512, 768), BF),
+    lse1=((2, 512, 128), F32),
+    lse2=((1024, 128), F32),
+    bias1=((2, 256, 384), F32),
+    bias2=((512, 128), F32),
+)
+
+
+def alias_late(r):
+    r.dq2 = r.act.at[0]
+    r.dfirst = r.act.at[1]
+    r.dqkv = r.gd
+
+
+def gather_kernel(*refs):
+    shards = refs[:9]
+    outs = refs[9:12]
+    sq, up, down, contrib, sib, psem, qsem, ssem, rsem, osem = refs[12:]
+    me = Place()
+    greet(me)
+    place_own(me, shards, sq, up, down, contrib, sib, psem, qsem)
+    gat = Gather(me, (sq, up, down), ssem, rsem)
+    for g in GROUPS:
+        gat.start(g)
+    for s in range(len(GROUPS) + 3):
+        if s < 5:
+            gat.step1(s)
+        if 0 <= s - 1 < 5:
+            gat.step2(s - 1)
+        if 0 <= s - 2 < 5:
+            gat.step3(s - 2)
+        if 0 <= s - 3 < 5:
+            gat.step4(s - 3)
+    for g in GROUPS:
+        gat.arrived(g)
+    copies = [
+        pltpu.make_async_copy(a, b, osem.at[i]) for i, (a, b) in enumerate(zip((sq, up, down), outs))
+    ]
+    for cp in copies:
+        cp.start()
+    for g in GROUPS:
+        gat.sent(g)
+    for cp in copies:
+        cp.wait()
+
+
+SQ = (7, 4, 2, 2, 48, 768)
+UP = (2, 2, 4, 2, 192, 384)
+DOWN = (4, 2, 96, 3072)
+
+
+def gather(shards):
+    return pl.pallas_call(
+        gather_kernel,
+        out_shape=[jax.ShapeDtypeStruct(s, BF) for s in (SQ, UP, DOWN)],
+        in_specs=[pl.BlockSpec(memory_space=pltpu.VMEM)] * 9,
+        out_specs=[pl.BlockSpec(memory_space=pl.ANY)] * 3,
+        scratch_shapes=[
+            pltpu.VMEM(SQ, BF),
+            pltpu.VMEM(UP, BF),
+            pltpu.VMEM(DOWN, BF),
+            pltpu.VMEM((7, 2, 48, 384), BF),
+            pltpu.VMEM((7, 48, 384), BF),
+            pltpu.SemaphoreType.DMA((1,)),
+            pltpu.SemaphoreType.DMA((1,)),
+            pltpu.SemaphoreType.DMA((5, 10)),
+            pltpu.SemaphoreType.DMA((5, 10)),
+            pltpu.SemaphoreType.DMA((3,)),
+        ],
+        compiler_params=pltpu.CompilerParams(
+            collective_id=0, has_side_effects=True, vmem_limit_bytes=56 * 2**20
+        ),
+    )(*shards)
+
+
+def vector_sum(me, vec, vbuf, vsem, wsem):
+    hops = [me.dev(me.own, c=1 - me.c), me.dev((1 - me.x, me.y)), me.dev((me.x, 1 - me.y))]
+    for i, d in enumerate(hops):
+        vbuf[i] = vec[...]
+        cp = rcopy(vbuf.at[i], vbuf.at[3 + i], vsem.at[i], wsem.at[i], d)
+        cp.start()
+        cp.wait()
+        vec[...] = vec[...] + vbuf[3 + i]
+    vbuf[6 + me.z] = vec[...]
+    cps = [
+        rcopy(
+            vbuf.at[6 + me.z], vbuf.at[6 + me.z], vsem.at[2 + k], wsem.at[2 + k], me.dev(me.own, z=me.peer(k))
+        )
+        for k in (1, 2, 3)
+    ]
+    for cp in cps:
+        cp.start()
+    for k in (1, 2, 3):
+        zz = lax.rem(me.z + 4 - k, 4)
+        rcopy(
+            vbuf.at[6 + zz], vbuf.at[6 + zz], vsem.at[2 + k], wsem.at[2 + k], me.dev(me.own, z=me.peer(k))
+        ).wait_recv()
+    for cp in cps:
+        cp.wait_send()
+    vec[...] = (vbuf[6] + vbuf[7]) + (vbuf[8] + vbuf[9])
+
+
+def scatter_kernel(*refs):
+    sq, up, down, vec_in = refs[:4]
+    o_sq, o_up, o_down, o_vec = refs[4:8]
+    s_sq, s_up, s_down = refs[8:11]
+    r1 = refs[11:14]
+    r2 = refs[14:17]
+    r3 = refs[17:20]
+    ssem, rsem, esem, vbuf, vsem, wsem, half = refs[20:]
+    me = Place()
+    greet(me)
+    sca = Scatter(me, (sq, up, down), (s_sq, s_up, s_down), r1, r2, r3, ssem, rsem)
+    order = (4, 3, 2, 1, 0)
+    for g in order:
+        sca.start(g)
+    for s in range(8):
+        if s < 5:
+            sca.step1(order[s])
+        if 0 <= s - 1 < 5:
+            sca.step2(order[s - 1])
+        if 0 <= s - 2 < 5:
+            sca.step3(order[s - 2])
+        if 0 <= s - 3 < 5:
+            g = order[s - 3]
+            total = sca.finish(g)
+            if g == 3:
+                o_up[...] = total
+            elif g == 4:
+                o_down[...] = total
+            else:
+                lo, hi = SQUARE[g]
+                half[lo:hi] = total
+    o_vec[...] = vec_in[...]
+    vector_sum(me, o_vec, vbuf, vsem, wsem)
+    swap = rcopy(half, o_sq.at[:, me.c], esem.at[0], esem.at[1], me.dev(me.own, c=1 - me.c))
+    swap.start()
+    o_sq[:, me.c] = half[...]
+    swap.wait_send()
+    rcopy(half, o_sq.at[:, 1 - me.c], esem.at[0], esem.at[1], me.dev(me.own, c=1 - me.c)).wait_recv()
+    for g in GROUPS:
+        sca.sent(g)
+
+
+def scatter(sq, up, down, vec):
+    def slots(n):
+        return [
+            pltpu.VMEM((n, 7, 4, 48, 384), BF),
+            pltpu.VMEM((n, 4, 192, 384), BF),
+            pltpu.VMEM((n, 4, 96, 768), BF),
+        ]
+
+    return pl.pallas_call(
+        scatter_kernel,
+        out_shape=[
+            jax.ShapeDtypeStruct((7, 2, 48, 384), F32),
+            jax.ShapeDtypeStruct((192, 384), F32),
+            jax.ShapeDtypeStruct((96, 768), F32),
+            jax.ShapeDtypeStruct(vec.shape, F32),
+        ],
+        in_specs=[pl.BlockSpec(memory_space=pltpu.VMEM)] * 4,
+        out_specs=[pl.BlockSpec(memory_space=pltpu.VMEM)] * 4,
+        scratch_shapes=[
+            pltpu.VMEM((7, 4, 2, 48, 768), BF),
+            pltpu.VMEM((2, 4, 2, 192, 384), BF),
+            pltpu.VMEM((4, 2, 96, 1536), BF),
+            *slots(2),
+            *slots(1),
+            pltpu.VMEM((3, 7, 48, 384), BF),
+            pltpu.VMEM((3, 192, 384), BF),
+            pltpu.VMEM((3, 96, 768), BF),
+            pltpu.SemaphoreType.DMA((5, 10)),
+            pltpu.SemaphoreType.DMA((5, 10)),
+            pltpu.SemaphoreType.DMA((2,)),
+            pltpu.VMEM((10, *vec.shape), F32),
+            pltpu.SemaphoreType.DMA((6,)),
+            pltpu.SemaphoreType.DMA((6,)),
+            pltpu.VMEM((7, 48, 384), F32),
+        ],
+        compiler_params=pltpu.CompilerParams(
+            collective_id=1, has_side_effects=True, vmem_limit_bytes=60 * 2**20
+        ),
+    )(sq, up, down, vec)
+
+
+def compute_kernel(*refs):
+    r = Refs()
+    (length, r.tokens, r.og, r.gains, r.shifts, r.pool, sq_in, up_in, down_in) = refs[:9]
+    (r.out, r.din, r.vec, sq_out, up_out, down_out) = refs[9:15]
+    r.sq, r.up, r.down = refs[15:18]
+    sem = refs[18]
+    for name, ref in zip(ACTIVE, refs[19:]):
+        setattr(r, name, ref)
+    alias_late(r)
+    loads = [pltpu.make_async_copy(a, b, sem.at[i]) for i, (a, b) in enumerate(((sq_in, r.sq), (up_in, r.up), (down_in, r.down)))]
+    for cp in loads:
+        cp.start()
+    set_masks(r, length[0])
+    loads[0].wait()
+    for m in range(3):
+        project(r, m)
+    for i in range(2):
+        project_pool(r, i)
+    level_one(r)
+    level_two(r)
+    first_norm(r)
+    loads[1].wait()
+    for j in range(4):
+        ffn_up(r, j)
+    loads[2].wait()
+    ffn_down_norm(r)
+    for j in range(4):
+        back_upper(r, j)
+    for j in range(4):
+        grad_down(r, j)
+    outs = [pltpu.make_async_copy(b, a, sem.at[i]) for i, (a, b) in enumerate(((sq_out, r.sq), (up_out, r.up), (down_out, r.down)))]
+    outs[2].start()
+    back_first_norm(r)
+    for j in range(4):
+        grad_up(r, j)
+    outs[1].start()
+    back_out(r)
+    back_level_two(r)
+    for i in range(2):
+        back_pool(r, i)
+    back_level_one(r)
+    for m in range(3):
+        finish_projection(r, m, r.dqkv[m])
+    outs[0].start()
+    r.din[...] = r.dr[...].astype(BF)
+    for cp in outs:
+        cp.wait()
+
+
+def compute(length, tokens, og, gains, shifts, pool, sq, up, down):
+    vmem = pl.BlockSpec(memory_space=pltpu.VMEM)
+    hbm = pl.BlockSpec(memory_space=pl.ANY)
+    return pl.pallas_call(
+        compute_kernel,
+        out_shape=[
+            jax.ShapeDtypeStruct((512, 768), BF),
+            jax.ShapeDtypeStruct((512, 768), BF),
+            jax.ShapeDtypeStruct((16, 768), F32),
+            jax.ShapeDtypeStruct(SQ, BF),
+            jax.ShapeDtypeStruct(UP, BF),
+            jax.ShapeDtypeStruct(DOWN, BF),
+        ],
+        in_specs=[pl.BlockSpec(memory_space=pltpu.SMEM)] + [vmem] * 5 + [hbm] * 3,
+        out_specs=[vmem] * 3 + [hbm] * 3,
+        scratch_shapes=[pltpu.VMEM(SQ, BF), pltpu.VMEM(UP, BF), pltpu.VMEM(DOWN, BF), pltpu.SemaphoreType.DMA((3,))]
+        + [pltpu.VMEM(*s) for s in ACTIVE.values()],
+        compiler_params=pltpu.CompilerParams(vmem_limit_bytes=58 * 2**20),
+    )(length, tokens, og, gains, shifts, pool, sq, up, down)
+
+
+def local_kernels(
+    tokens,
+    doc_lengths,
+    w_query,
+    w_key,
+    w_value,
+    w_query2,
+    w_key2,
+    w_value2,
+    w_out,
+    w_up,
+    w_down,
+    norm_gains,
+    norm_shifts,
+    pool_kernels,
+    out_grad,
+):
+    shards = (w_query, w_key, w_value, w_key2, w_value2, w_query2, w_out, w_up, w_down)
+    sq, up, down = gather(shards)
+    activations, d_tokens, vec, g_sq, g_up, g_down = compute(
+        doc_lengths, tokens, out_grad, norm_gains, norm_shifts, pool_kernels, sq, up, down
+    )
+    o_sq, o_up, o_down, o_vec = scatter(g_sq, g_up, g_down, vec)
+    core = lax.rem(lax.axis_index("dp"), 2)
+    mine = lax.dynamic_slice_in_dim(o_sq.reshape(7, 96, 384), core * 192, 192, 2).transpose(0, 2, 1)
+    return (
+        activations,
+        d_tokens,
+        *[mine[i] for i in (0, 1, 2, 5, 3, 4, 6)],
+        o_up,
+        o_down.T,
+        o_vec[0:2],
+        o_vec[2:4],
+        o_vec[4:14].reshape(2, 5, 768),
     )
 
 
@@ -405,8 +1252,9 @@
 
 
 def solution(mesh):
+    fits = mesh.shape["dp"] == 4 and mesh.shape["fsdp"] == 8
     return jax.shard_map(
-        local,
+        local_kernels if fits else local,
         mesh=mesh,
         in_specs=(
             P(("dp", "fsdp"), None),

time: 1330 us -> 308 us (0.23)
  waiting for transfers between devices: 691 us -> 0 us
  Pallas kernels: 0 us -> 292 us
  blocking collectives: 219 us -> 0 us
  matrix products: 209 us -> 0 us
  local copies, waits for them, and re-layouts: 131 us -> 10.9 us
  other arithmetic: 48.3 us -> 0 us
  between operations: 16.8 us -> 1.78 us
    reduce_scatter x10 -> x0, waiting for transfers between devices: 404 us -> none  [the longest x1 97.4 us: reduce_columns_first(): lax.psum_scatter(grads_all[8].astype(jnp.bfloat16), 'fsdp', scatter_dimen...]
    pallas_call x0 -> x3, Pallas kernels: none -> 292 us  [the longest x1 118 us: scatter(): pl.pallas_call(scatter_kernel, out_shape=[jax.ShapeDtypeStruct((7, 2, 48,...]
    dot_general x111 -> x0, matrix products: 209 us -> none  [the longest x9 33.7 us: inner_rows(): lax.dot_general(left_mat, right_mat, (((0,), (0,)), ((), ())), preferred_...]
    unnamed x37 -> x0, waiting for transfers between devices: 190 us -> none
    all_gather x7 -> x0, blocking collectives: 175 us -> none  [the longest x1 26.2 us: gather_first(): lax.all_gather(shards[4], 'fsdp', axis=1, tiled=True)]
    all_gather x11 -> x0, waiting for transfers between devices: 97.5 us -> none  [the longest x1 32.8 us: gather_first(): lax.all_gather(column_parts[7], 'dp', axis=0, tiled=True)]
    unnamed x233 -> x8, local copies, waits for them, and re-layouts: 63.8 us -> 6.42 us
    psum x1 -> x0, blocking collectives: 43.2 us -> none  [local(): lax.psum((gain_stack, shift_stack, pool_stack), ('dp', 'fsdp'))]
  transfers between devices with their start and end apart: 29 -> 0, of which waited for: 19 -> 0; matrix products, arithmetic and copies ran while one was open for 26% -> 0% of each run, Pallas kernels for 0% -> 0%
where the time goes in v1:
time: 308 us; the launch traced here: 304 us
  Pallas kernels  292 us (95%)
  local copies, waits for them, and re-layouts  10.9 us (4%)
    pallas_call x1, Pallas kernels, scatter(): pl.pallas_call(scatter_kernel, out_shape=[jax.ShapeDtypeStruct((7, 2, 48,...  118 us
    pallas_call x1, Pallas kernels, gather(): pl.pallas_call(gather_kernel, out_shape=[jax.ShapeDtypeStruct(s, BF) for...  99.3 us
    pallas_call x1, Pallas kernels, compute(): pl.pallas_call(compute_kernel, out_shape=[jax.ShapeDtypeStruct((512, 768)...  74.3 us
    unnamed x8, local copies, waits for them, and re-layouts  6.42 us

profile of v1, /device:TPU:1, one launch (start us, length us, event | category | flops | bytes accessed | tf_op | source)
XLA Modules:
  0.0 304.3 jit_solution(17144312524449772861)
XLA Ops:
  1.3 1.4 copy.34.refs_5_
  2.7 1.7 copy.33.refs_8_
  4.4 99.3 %shard_map.254 = (bf16[7,4,2,2,48,768]{5,4,3,2,1,0:T(8,128)(2,1)}, bf16[2,2,4,2,192,384]{5,4,3,2,1,0:T(8,128)(2,1)}, bf16[4,2,96,3072]{3,2,1,0:T(8,128)(2,1)}) custom-call(bf16[192,96]{1,0:T(8,128)(2,1)} %refs_0_.2, bf16[192,96]{1,0:T(8,128)(2,1)} %refs_1_.2, bf16[192,96]{1,0:T(8,128)(2,1)} %refs_2_.2, bf16[192,96]{1,0:T(8,128)(2,1)} %refs_3_.2, ...), custom_call_target="tpu_custom_call" | custom-call | tf_op jit(solution)/shard_map/pallas_call | solution.py:855
  103.7 74.3 %shard_map.255 = (bf16[512,768]{1,0:T(8,128)(2,1)}, bf16[512,768]{1,0:T(8,128)(2,1)}, f32[16,768]{1,0:T(8,128)}, bf16[7,4,2,2,48,768]{5,4,3,2,1,0:T(8,128)(2,1)}...) custom-call(s32[1]{0:T(128)S(6)} %copy.40.refs_0_, bf16[512,768]{1,0:T(8,128)(2,1)} %refs_1_.3, ...), custom_call_target="tpu_custom_call" | custom-call | tf_op jit(solution)/shard_map/pallas_call | solution.py:1040
  178.0 118.0 %shard_map.256 = (f32[7,2,48,384]{3,2,1,0:T(8,128)}, f32[192,384]{1,0:T(8,128)}, f32[96,768]{1,0:T(8,128)}, f32[16,768]{1,0:T(8,128)}) custom-call(bf16[7,4,2,2,48,768]{5,4,3,2,1,0:T(8,128)(2,1)} %get-tuple-element.32.refs_0_, bf16[2,2,4,2,192,384]{5,4,3,2,1,0:T(8,128)(2,1)} %get-tuple-element.33.refs_1_, ...), custom_call_target="tpu_custom_call" | custom-call | tf_op jit(solution)/shard_map/pallas_call | solution.py:955
  296.0 0.0 copy-start
  296.0 1.4 constant_dynamic-slice_fusion
  297.4 0.3 copy.37
  297.7 0.8 slice_bitcast_fusion
  298.5 1.4 fusion
  300.0 0.8 slice.39
  300.8 0.6 copy.36
  301.4 1.7 copy.41
  303.1 0.0 copy-done
  303.1 0.7 copy.42
  (1 shorter events, 0.0 us)
Async XLA Ops:
  296.0 7.1 %copy-start = (f32[96,768]{1,0:T(8,128)S(1)}, f32[96,768]{1,0:T(8,128)}, u32[]{:S(2)}) copy-start(f32[96,768]{1,0:T(8,128)} %get-tuple-element.38) | copy-start | bytes 884740

commit v2 on v0

--- a/solution.py
+++ b/solution.py
@@ -3,6 +3,8 @@
 import jax
 import jax.numpy as jnp
 from jax import lax
+from jax.experimental import pallas as pl
+from jax.experimental.pallas import tpu as pltpu
 from jax.sharding import PartitionSpec as P
 
 HEADS = 12
@@ -242,6 +244,1005 @@
         lax.psum_scatter(
             column_sums[8].astype(jnp.bfloat16), "dp", scatter_dimension=0, tiled=True
         ).astype(jnp.float32),
+    )
+
+
+MESH = pl.DeviceIdType.MESH
+BF = jnp.bfloat16
+F32 = jnp.float32
+
+GROUPS = (
+    ("s", 0, 1),
+    ("s", 1, 3),
+    ("s", 3, 5),
+    ("s", 5, 7),
+    ("u", 0, 96),
+    ("u", 96, 192),
+    ("d", 0, 48),
+    ("d", 48, 96),
+)
+N_GROUPS = len(GROUPS)
+SQ = (7, 4, 2, 2, 48, 768)
+UP = (2, 2, 4, 2, 192, 384)
+DOWN = (4, 2, 2, 2, 96, 768)
+
+
+class Place:
+    def __init__(self):
+        dp = lax.axis_index("dp")
+        fs = lax.axis_index("fsdp")
+        self.y = lax.div(dp, 2)
+        self.c = lax.rem(dp, 2)
+        self.z = lax.div(fs, 2)
+        self.x = lax.rem(fs, 2)
+        c, x, y = self.c, self.x, self.y
+        self.p1 = ((1 - c) * (1 - x) + c * x, (1 - c) * y + c * (1 - y))
+        self.p2 = ((1 - c) * x + c * (1 - x), (1 - c) * (1 - y) + c * y)
+        self.own = (x, y)
+        self.diag = (1 - x, 1 - y)
+
+    def dev(self, xy, z=None, c=None):
+        z = self.z if z is None else z
+        c = self.c if c is None else c
+        return (xy[1] * 2 + c, z * 2 + xy[0])
+
+    def sibling(self):
+        return self.dev(self.own, c=1 - self.c)
+
+    def peer(self, k):
+        return lax.rem(self.z + k, 4)
+
+    def everyone(self):
+        return [self.sibling(), self.dev(self.p1), self.dev(self.p2)] + [
+            self.dev(self.own, z=self.peer(k)) for k in (1, 2, 3)
+        ]
+
+
+def greet(me):
+    bar = pltpu.get_barrier_semaphore()
+    for d in me.everyone():
+        pl.semaphore_signal(bar, inc=1, device_id=d, device_id_type=MESH)
+    pl.semaphore_wait(bar, 6)
+
+
+def square_lanes(y):
+    return pl.ds(pl.multiple_of(y * 384, 128), 384)
+
+
+def blocks(refs, g, xy, c, z=slice(None)):
+    sq, up, down = refs
+    x, y = xy
+    kind, lo, hi = GROUPS[g]
+    if kind == "s":
+        return sq.at[lo:hi, z, x, c, :, square_lanes(y)]
+    if kind == "u":
+        return up.at[y, c, z, x, lo:hi]
+    return down.at[z, x, y, c, lo:hi]
+
+
+def rcopy(src, dst, ssem, rsem, dev):
+    return pltpu.make_async_remote_copy(
+        src_ref=src, dst_ref=dst, send_sem=ssem, recv_sem=rsem, device_id=dev, device_id_type=MESH
+    )
+
+
+class Gather:
+    def __init__(self, me, refs, ssem, rsem):
+        self.me, self.refs, self.ssem, self.rsem = me, refs, ssem, rsem
+
+    def copy(self, g, i, incoming=False):
+        me = self.me
+        ss, rs = self.ssem.at[g, i], self.rsem.at[g, i]
+        side = 1 if incoming else 0
+        c = me.c
+        ways = ((me.own, me.p1), (me.own, me.p2), (me.p1, me.diag))
+        if i < 3:
+            b = blocks(self.refs, g, ways[i][side], c, me.z)
+            return rcopy(b, b, ss, rs, me.dev(me.p1 if i == 0 else me.p2))
+        if i < 6:
+            k = i - 2
+            z = lax.rem(me.z + 4 - k, 4) if incoming else me.z
+            b = blocks(self.refs, g, me.own, c, z)
+            return rcopy(b, b, ss, rs, me.dev(me.own, z=me.peer(k)))
+        if i < 10:
+            cc = 1 - c if incoming else c
+            what = ((me.own, me.own), (me.p1, me.p2), (me.p2, me.p1), (me.diag, me.diag))[i - 6][side]
+            b = blocks(self.refs, g, what, cc)
+            return rcopy(b, b, ss, rs, me.sibling())
+        way, k = (i - 10) // 3, (i - 10) % 3 + 1
+        b = blocks(self.refs, g, ways[way][side], c, lax.rem(me.z + 4 - k, 4))
+        return rcopy(b, b, ss, rs, me.dev(me.p1 if way == 0 else me.p2))
+
+    def go(self, g, *which):
+        for i in which:
+            self.copy(g, i).start()
+
+    def got(self, g, *which):
+        for i in which:
+            self.copy(g, i, True).wait_recv()
+
+    def start(self, g):
+        self.go(g, 0, 1, 3, 4, 5)
+
+    def step0(self, g):
+        self.got(g, 0)
+        self.go(g, 2)
+
+    def step1(self, g):
+        for k in range(3):
+            self.got(g, 3 + k)
+            self.go(g, 13 + k, 10 + k)
+        self.go(g, 6)
+
+    def step2(self, g):
+        for k in range(3):
+            self.got(g, 10 + k)
+            self.go(g, 16 + k)
+        self.go(g, 7)
+
+    def step3(self, g):
+        self.got(g, 1, 13, 14, 15)
+        self.go(g, 8)
+
+    def step4(self, g):
+        self.got(g, 2, 16, 17, 18)
+        self.go(g, 9)
+
+    def arrived(self, g):
+        self.got(g, 6, 7, 8, 9)
+
+    def sent(self, g):
+        for i in range(19):
+            self.copy(g, i).wait_send()
+
+
+class Scatter:
+    def __init__(self, me, refs, sib, r1, r2, r3, ssem, rsem):
+        self.me, self.refs, self.sib = me, refs, sib
+        self.r1, self.r2, self.r3 = r1, r2, r3
+        self.ssem, self.rsem = ssem, rsem
+
+    def sib_view(self, g, xy, z=slice(None)):
+        sq, up, down = self.sib
+        x, y = xy
+        kind, lo, hi = GROUPS[g]
+        if kind == "s":
+            return sq.at[lo:hi, z, x, :, square_lanes(y)]
+        if kind == "u":
+            return up.at[y, z, x, lo:hi]
+        return down.at[z, x, y, lo:hi]
+
+    def slot(self, bufs, g, i):
+        kind, lo, hi = GROUPS[g]
+        if kind == "s":
+            return bufs[0].at[i, lo:hi]
+        buf = bufs[1 if kind == "u" else 2]
+        return buf.at[i, :, lo:hi] if len(buf.shape) == 4 else buf.at[i, lo:hi]
+
+    def copy(self, g, i):
+        me = self.me
+        c = me.c
+        ss, rs = self.ssem.at[g, i], self.rsem.at[g, i]
+        if i < 4:
+            what = (me.p1, me.diag, me.p2, me.own)[i]
+            return rcopy(blocks(self.refs, g, what, 1 - c), self.sib_view(g, what), ss, rs, me.sibling())
+        if i < 6:
+            src = blocks(self.refs, g, (me.diag, me.p2)[i - 4], c)
+            return rcopy(src, self.slot(self.r1, g, i - 4), ss, rs, me.dev(me.p2))
+        if i == 6:
+            return rcopy(blocks(self.refs, g, me.p1, c), self.slot(self.r2, g, 0), ss, rs, me.dev(me.p1))
+        k = i - 6
+        src = blocks(self.refs, g, me.own, c, me.peer(k))
+        return rcopy(src, self.slot(self.r3, g, k - 1), ss, rs, me.dev(me.own, z=me.peer(k)))
+
+    def go(self, g, *which):
+        for i in which:
+            self.copy(g, i).start()
+
+    def got(self, g, i):
+        self.copy(g, i).wait_recv()
+
+    def add(self, here, *others):
+        total = here[...].astype(F32)
+        for other in others:
+            total = total + other[...].astype(F32)
+        here[...] = total.astype(BF)
+
+    def start(self, g):
+        self.go(g, 0, 1, 2, 3)
+
+    def step1(self, g):
+        me = self.me
+        for i, what, out in ((1, me.diag, 4), (0, me.p2, 5)):
+            self.got(g, i)
+            self.add(blocks(self.refs, g, what, me.c), self.sib_view(g, what))
+            self.go(g, out)
+
+    def step2(self, g):
+        me = self.me
+        self.got(g, 2)
+        self.got(g, 4)
+        here = blocks(self.refs, g, me.p1, me.c)
+        self.add(here, self.sib_view(g, me.p1), self.slot(self.r1, g, 0))
+        self.go(g, 6)
+
+    def step3(self, g):
+        me = self.me
+        self.got(g, 3)
+        self.got(g, 5)
+        self.got(g, 6)
+        here = blocks(self.refs, g, me.own, me.c)
+        self.add(here, self.sib_view(g, me.own), self.slot(self.r1, g, 1), self.slot(self.r2, g, 0))
+        self.go(g, 7, 8, 9)
+
+    def finish(self, g):
+        me = self.me
+        total = blocks(self.refs, g, me.own, me.c, me.z)[...].astype(F32)
+        for k in (1, 2, 3):
+            self.got(g, 6 + k)
+            total = total + self.slot(self.r3, g, k - 1)[...].astype(F32)
+        return total
+
+    def sent(self, g):
+        for i in range(10):
+            self.copy(g, i).wait_send()
+
+
+class VectorSum:
+    def __init__(self, me, vec, buf, ssem, rsem):
+        self.me, self.vec, self.buf, self.ssem, self.rsem = me, vec, buf, ssem, rsem
+        self.hops = [me.sibling(), me.dev((1 - me.x, me.y)), me.dev((me.x, 1 - me.y))]
+
+    def hop(self, i):
+        b = self.buf
+        return rcopy(b.at[i], b.at[3 + i], self.ssem.at[i], self.rsem.at[i], self.hops[i])
+
+    def send(self, i):
+        self.buf[i] = self.vec[...]
+        self.hop(i).start()
+
+    def take(self, i):
+        self.hop(i).wait()
+        self.vec[...] = self.vec[...] + self.buf[3 + i]
+
+    def zcopy(self, k, incoming):
+        me = self.me
+        b = self.buf.at[6 + (lax.rem(me.z + 4 - k, 4) if incoming else me.z)]
+        return rcopy(b, b, self.ssem.at[2 + k], self.rsem.at[2 + k], me.dev(me.own, z=me.peer(k)))
+
+    def send_z(self):
+        self.buf[6 + self.me.z] = self.vec[...]
+        for k in (1, 2, 3):
+            self.zcopy(k, False).start()
+
+    def take_z(self):
+        for k in (1, 2, 3):
+            self.zcopy(k, True).wait_recv()
+        for k in (1, 2, 3):
+            self.zcopy(k, False).wait_send()
+        b = self.buf
+        self.vec[...] = (b[6] + b[7]) + (b[8] + b[9])
+
+
+def place_squares(me, shards, sq, room, ssem, rsem):
+    rows = lax.broadcasted_iota(jnp.int32, (192, 384), 0)
+    lanes = lax.broadcasted_iota(jnp.int32, (192, 384), 1)
+    spot = jnp.where(lanes == rows + me.c * 192, 1.0, 0.0).astype(BF)
+    for m in range(7):
+        t = dg(shards[m][...], spot, 0, 0).astype(BF)
+        for half in range(2):
+            room[half, 48 * m : 48 * m + 48, 0:384] = t[48 * half : 48 * half + 48]
+    area = (pl.ds(0, 336), pl.ds(0, 384))
+    swap = rcopy(room.at[(1 - me.c, *area)], room.at[(2, *area)], ssem, rsem, me.sibling())
+    swap.start()
+    swap.wait()
+    for m in range(7):
+        rows = slice(48 * m, 48 * m + 48)
+        both = room[me.c, rows, 0:384].astype(F32) + room[2, rows, 0:384].astype(F32)
+        sq[m, me.z, me.x, me.c, :, square_lanes(me.y)] = both.astype(BF)
+
+
+GAIN, SHIFT, POOL = 0, 2, 4
+
+
+def dg(a, b, ca, cb):
+    return lax.dot_general(a, b, (((ca,), (cb,)), ((), ())), preferred_element_type=F32)
+
+
+def weight(r, m):
+    return r.sq[m].reshape(768, 768)
+
+
+def weight_up(r, j):
+    left = r.up[:, :, j, 0].reshape(768, 384)
+    right = r.up[:, :, j, 1].reshape(768, 384)
+    return jnp.concatenate([left, right], axis=1)
+
+
+def weight_down(r, y, c):
+    return r.down[:, :, y, c].reshape(768, 768)
+
+
+def set_masks(r, length):
+    for i in range(2):
+        row = lax.broadcasted_iota(jnp.int32, (256, 384), 0) + 256 * i
+        col = lax.broadcasted_iota(jnp.int32, (256, 384), 1) + 128 * i
+        ok = (jnp.abs(row - col) <= WIN) & ((row >= length) == (col >= length))
+        r.bias1[i] = jnp.where(ok, 0.0, -1e30)
+    row = lax.broadcasted_iota(jnp.int32, (512, 128), 0)
+    col = lax.broadcasted_iota(jnp.int32, (512, 128), 1) * STRIDE
+    ok = (jnp.abs(row - col) <= PWIN // 2) & ((row >= length) == (col >= length))
+    r.bias2[...] = jnp.where(ok, 0.0, -1e30)
+
+
+def low_lanes(rows):
+    return lax.broadcasted_iota(jnp.int32, (rows, 128), 1) < HD
+
+
+def two_heads(pair):
+    low = low_lanes(pair.shape[0])
+    zero = jnp.zeros_like(pair)
+    return jnp.concatenate([jnp.where(low, pair, zero), jnp.where(low, zero, pair)], axis=0)
+
+
+def side_by_side(stacked):
+    n = stacked.shape[0] // 2
+    return jnp.where(low_lanes(n), stacked[:n], stacked[n:])
+
+
+def pair_lanes(p):
+    return pl.ds(pl.multiple_of(p * 128, 128), 128)
+
+
+def softmax_out(scores, bias, values, lse_ref, p):
+    scores = scores + jnp.concatenate([bias, bias], axis=0)
+    highest = jnp.max(scores, axis=-1, keepdims=True)
+    terms = jnp.exp(scores - highest)
+    summed = jnp.sum(terms, axis=-1, keepdims=True)
+    probs = (terms * (1.0 / summed)).astype(BF)
+    lane = lax.broadcasted_iota(jnp.int32, lse_ref.shape, 1)
+    lse_ref[...] = jnp.where(lane == p, highest + jnp.log(summed), lse_ref[...])
+    return side_by_side(dg(probs, values, 1, 0))
+
+
+def scores_of(query, keys):
+    scaled = two_heads(query * jnp.asarray(0.125, BF))
+    return scaled, dg(scaled, keys, 1, 1)
+
+
+def softmax_back(scores, bias, lse_ref, p, grad, values):
+    scores = scores + jnp.concatenate([bias, bias], axis=0)
+    lane = lax.broadcasted_iota(jnp.int32, lse_ref.shape, 1)
+    lse = jnp.sum(jnp.where(lane == p, lse_ref[...], 0.0), axis=-1, keepdims=True)
+    probs = jnp.exp(scores - lse)
+    grad_probs = dg(grad, values, 1, 1)
+    row_terms = jnp.sum(probs * grad_probs, axis=-1, keepdims=True)
+    return probs.astype(BF), (probs * (grad_probs - row_terms)).astype(BF)
+
+
+def project(r, lo, hi):
+    @pl.loop(lo, hi)
+    def _(m):
+        r.qkv[m] = dg(r.tokens[...], weight(r, m), 1, 1).astype(BF)
+
+
+def project_pool(r, i):
+    full = None
+    for l in range(6):
+        lanes = slice(l * 128, l * 128 + 128)
+        if l % 3 == 0:
+            full = dg(r.tokens[...], r.sq[3 + i, 2 * (l // 3) : 2 * (l // 3) + 2].reshape(384, 768), 1, 1)
+        r.kt[i, l, 0:8] = jnp.zeros((8, 128), F32)
+        r.kt[i, l, 520:528] = jnp.zeros((8, 128), F32)
+        r.kt[i, l, 8:520] = full[:, (l % 3) * 128 : (l % 3) * 128 + 128]
+        total = None
+        for t in range(5):
+            term = r.pool[t, i : i + 1, lanes] * r.kt[i, l, pl.ds(6 + t, 128, stride=STRIDE), :]
+            total = term if total is None else total + term
+        r.kp[i, :, lanes] = total.astype(BF)
+
+
+def at_steps(p, hooks):
+    for at, hook in (hooks or {}).items():
+        pl.when(p == at)(hook)
+
+
+def level_one(r, hooks=None):
+    @pl.loop(0, HEADS // 2)
+    def _(p):
+        at_steps(p, hooks)
+        lanes = pair_lanes(p)
+        for i in range(2):
+            rows, cols = pl.ds(256 * i, 256), pl.ds(128 * i, 384)
+            _, scores = scores_of(r.qkv[0, rows, lanes], r.qkv[1, cols, lanes])
+            out = softmax_out(scores, r.bias1[i], r.qkv[2, cols, lanes], r.lse.at[pl.ds(512 * i, 512)], p)
+            r.first[rows, lanes] = out.astype(BF)
+
+
+def level_two(r):
+    r.q2[...] = dg(r.first[...], weight(r, 5), 1, 1).astype(BF)
+
+    @pl.loop(0, HEADS // 2)
+    def _(p):
+        lanes = pair_lanes(p)
+        _, scores = scores_of(r.q2[:, lanes], r.kp[0, :, lanes])
+        out = softmax_out(scores, r.bias2[...], r.kp[1, :, lanes], r.lse, p + HEADS // 2)
+        r.mixed[:, lanes] = (r.first[:, lanes].astype(F32) + out).astype(BF)
+
+
+def norm_parts(x):
+    average = jnp.mean(x, axis=-1, keepdims=True)
+    centred = x - average
+    inverse = lax.rsqrt(jnp.mean(centred * centred, axis=-1, keepdims=True) + 1e-05)
+    return centred * inverse, inverse
+
+
+def norm_back(n, inverse, gain, grad):
+    scaled = grad * gain
+    return (
+        scaled - jnp.mean(scaled, axis=-1, keepdims=True) - n * jnp.mean(scaled * n, axis=-1, keepdims=True)
+    ) * inverse
+
+
+def first_norm(r):
+    r.acc[...] = dg(r.mixed[...], weight(r, 6), 1, 1)
+
+    @pl.loop(0, 4)
+    def _(i):
+        rows = pl.ds(pl.multiple_of(i * 128, 128), 128)
+        n, inverse = norm_parts(r.tokens[rows].astype(F32) + r.acc[rows])
+        r.n1[rows] = n
+        r.inv1[rows] = inverse
+        r.hlow[rows] = (n * r.gains[0:1] + r.shifts[0:1]).astype(BF)
+
+
+def ffn_up(r):
+    k = math.sqrt(2.0 / math.pi)
+
+    @pl.loop(0, 4)
+    def _(j):
+        for i in range(2):
+            rows = pl.ds(256 * i, 256)
+            u = dg(r.hlow[rows], weight_up(r, j), 1, 0)
+            square = u * u
+            t = jnp.tanh(k * u * (1.0 + 0.044715 * square))
+            half = 0.5 * (1.0 + t)
+            r.act[j, rows] = (u * half).astype(BF)
+            slope = half + (0.5 * k) * u * (1.0 - t * t) * (1.0 + (3 * 0.044715) * square)
+            r.gd[j, rows] = slope.astype(BF)
+
+
+def ffn_down_norm(r):
+    @pl.loop(0, 2)
+    def _(i):
+        rows = pl.ds(pl.multiple_of(256 * i, 256), 256)
+        total = dg(r.act[0, rows], weight_down(r, 0, 0), 1, 1)
+        for j in range(1, 4):
+            total = total + dg(r.act[j, rows], weight_down(r, j // 2, j % 2), 1, 1)
+        r.acc[rows] = total
+
+    r.vec[...] = jnp.zeros_like(r.vec)
+
+    @pl.loop(0, 4)
+    def _(i):
+        rows = pl.ds(pl.multiple_of(i * 128, 128), 128)
+        hidden = r.n1[rows] * r.gains[0:1] + r.shifts[0:1]
+        n, inverse = norm_parts(hidden + r.acc[rows])
+        grad = r.og[rows].astype(F32)
+        r.og[rows] = (n * r.gains[1:2] + r.shifts[1:2]).astype(BF)
+        r.vec[GAIN + 1 : GAIN + 2] += jnp.sum(grad * n, axis=0, keepdims=True)
+        r.vec[SHIFT + 1 : SHIFT + 2] += jnp.sum(grad, axis=0, keepdims=True)
+        d = norm_back(n, inverse, r.gains[1:2], grad)
+        r.dr[rows] = d
+        r.dlow[rows] = d.astype(BF)
+
+
+def back_down(r, c):
+    @pl.loop(0, 2)
+    def _(y):
+        j = y * 2 + c
+        t = dg(r.dlow[...], weight_down(r, y, c), 1, 0)
+        r.gd[j] = (r.gd[j].astype(F32) * t).astype(BF)
+        for i in range(2):
+            g = dg(r.dlow[:, 384 * i : 384 * i + 384], r.act[j], 0, 0).astype(BF)
+            r.down[2 * i : 2 * i + 2, :, y, c] = g.reshape(2, 2, 96, 768)
+
+
+def back_first_norm(r):
+    @pl.loop(0, 2)
+    def _(i):
+        rows = pl.ds(pl.multiple_of(256 * i, 256), 256)
+        total = r.dr[rows]
+        for j in range(4):
+            total = total + dg(r.gd[j, rows], weight_up(r, j), 1, 1)
+        r.acc[rows] = total
+
+    @pl.loop(0, 4)
+    def _(i):
+        rows = pl.ds(pl.multiple_of(i * 128, 128), 128)
+        grad = r.acc[rows]
+        n = r.n1[rows]
+        r.vec[GAIN : GAIN + 1] += jnp.sum(grad * n, axis=0, keepdims=True)
+        r.vec[SHIFT : SHIFT + 1] += jnp.sum(grad, axis=0, keepdims=True)
+        d = norm_back(n, r.inv1[rows], r.gains[0:1], grad)
+        r.dr[rows] = d
+        r.dlow[rows] = d.astype(BF)
+
+
+def grad_up(r):
+    @pl.loop(0, 4)
+    def _(j):
+        for i in range(2):
+            g = dg(r.hlow[:, 384 * i : 384 * i + 384], r.gd[j], 0, 0).astype(BF)
+            for x in range(2):
+                r.up[i, :, j, x] = g[:, x * 384 : (x + 1) * 384].reshape(2, 192, 384)
+
+
+def set_grad(r, m, left, right):
+    for i in range(2):
+        g = dg(left[:, 384 * i : 384 * i + 384], right, 0, 0).astype(BF)
+        r.sq[m, 2 * i : 2 * i + 2] = g.reshape(2, 2, 2, 48, 768)
+
+
+def back_out(r):
+    r.acc[...] = dg(r.dlow[...], weight(r, 6), 1, 0)
+    set_grad(r, 6, r.dlow[...], r.mixed[...])
+
+
+def back_level_two(r, hooks=None):
+    @pl.loop(0, HEADS // 2)
+    def _(p):
+        at_steps(p, hooks)
+        lanes = pair_lanes(p)
+        scaled, scores = scores_of(r.q2[:, lanes], r.kp[0, :, lanes])
+        grad = two_heads(r.acc[:, lanes].astype(BF))
+        probs, grad_scores = softmax_back(
+            scores, r.bias2[...], r.lse, p + HEADS // 2, grad, r.kp[1, :, lanes]
+        )
+        r.dpool[1][0:128, lanes] = dg(probs, grad, 0, 0).astype(BF).astype(F32)
+        r.dpool[0][0:128, lanes] = dg(grad_scores, scaled, 0, 0).astype(BF).astype(F32)
+        r.dq2[:, lanes] = (side_by_side(dg(grad_scores, r.kp[0, :, lanes], 1, 0)) * 0.125).astype(BF)
+
+    r.dfirst[...] = (r.acc[...] + dg(r.dq2[...], weight(r, 5), 1, 0)).astype(BF)
+    set_grad(r, 5, r.dq2[...], r.first[...])
+
+
+def back_pool(r, i):
+    r.dpool[i][128:136] = jnp.zeros((8, 768), F32)
+    for l in range(6):
+        lanes = slice(l * 128, l * 128 + 128)
+        here = r.dpool[i][0:128, lanes]
+        after = r.dpool[i][1:129, lanes]
+        for t in range(5):
+            term = here * r.kt[i, l, pl.ds(6 + t, 128, stride=STRIDE), :]
+            at = POOL + 2 * t + i
+            r.vec[at : at + 1, lanes] = jnp.sum(term, axis=0, keepdims=True)
+        k = [r.pool[t, i : i + 1, lanes] for t in range(5)]
+        r.kt[i, l, pl.ds(8, 128, stride=STRIDE), :] = k[2] * here
+        r.kt[i, l, pl.ds(9, 128, stride=STRIDE), :] = k[3] * here
+        r.kt[i, l, pl.ds(10, 128, stride=STRIDE), :] = k[4] * here + k[0] * after
+        r.kt[i, l, pl.ds(11, 128, stride=STRIDE), :] = k[1] * after
+    grad = jnp.concatenate([r.kt[i, l, 8:520].astype(BF) for l in range(6)], axis=1)
+    finish_projection(r, 3 + i, grad)
+
+
+def finish_projection(r, m, grad):
+    r.dr[...] = r.dr[...] + dg(grad, weight(r, m), 1, 0)
+    set_grad(r, m, grad, r.tokens[...])
+
+
+def back_level_one(r, hooks=None):
+    @pl.loop(0, HEADS)
+    def _(step):
+        at_steps(step, hooks)
+        p, i = lax.div(step, 2), lax.rem(step, 2)
+        lanes = pair_lanes(p)
+        rows = pl.ds(pl.multiple_of(256 * i, 256), 256)
+        cols = pl.ds(pl.multiple_of(128 * i, 128), 384)
+        scaled, scores = scores_of(r.qkv[0, rows, lanes], r.qkv[1, cols, lanes])
+        grad = two_heads(r.dfirst[rows, lanes])
+        stacked = r.lse.at[pl.ds(pl.multiple_of(512 * i, 512), 512)]
+        probs, grad_scores = softmax_back(scores, r.bias1[i], stacked, p, grad, r.qkv[2, cols, lanes])
+
+        @pl.when(i == 0)
+        def _():
+            r.acc[:, 0:256] = jnp.zeros((512, 256), F32)
+
+        r.acc[cols, 0:128] += dg(grad_scores, scaled, 0, 0)
+        r.acc[cols, 128:256] += dg(probs, grad, 0, 0)
+        dq = side_by_side(dg(grad_scores, r.qkv[1, cols, lanes], 1, 0)) * 0.125
+        r.dqkv[0, rows, lanes] = dq.astype(BF)
+
+        @pl.when(i == 1)
+        def _():
+            r.dqkv[1, :, lanes] = r.acc[:, 0:128].astype(BF)
+            r.dqkv[2, :, lanes] = r.acc[:, 128:256].astype(BF)
+
+
+class Refs:
+    pass
+
+
+ACTIVE = dict(
+    qkv=((3, 512, 768), BF),
+    kt=((2, 6, 528, 128), F32),
+    kp=((2, 128, 768), BF),
+    first=((512, 768), BF),
+    q2=((512, 768), BF),
+    mixed=((512, 768), BF),
+    n1=((512, 768), F32),
+    inv1=((512, 1), F32),
+    hlow=((512, 768), BF),
+    act=((4, 512, 768), BF),
+    gd=((4, 512, 768), BF),
+    dr=((512, 768), F32),
+    acc=((512, 768), F32),
+    dlow=((512, 768), BF),
+    lse=((1024, 128), F32),
+    bias1=((2, 256, 384), F32),
+    bias2=((512, 128), F32),
+)
+
+
+def alias_late(r):
+    r.dq2 = r.act.at[0]
+    r.dfirst = r.act.at[1]
+    r.dqkv = r.gd
+    r.dpool = (r.n1.at[pl.ds(0, 136)], r.n1.at[pl.ds(256, 136)])
+
+
+def slots(n):
+    return dict(
+        sq=((n, 7, 4, 48, 384), BF),
+        up=((n, 4, 192, 384), BF),
+        down=((n, 4, 96, 768), BF),
+    )
+
+
+BUFFERS = dict(
+    tokens=((512, 768), BF),
+    og=((512, 768), BF),
+    gains=((2, 768), F32),
+    shifts=((2, 768), F32),
+    pool=((5, 2, 768), F32),
+    shards=((7, 192, 96), BF),
+    sq=(SQ, BF),
+    up=(UP, BF),
+    down=(DOWN, BF),
+    s_sq=((7, 4, 2, 48, 768), BF),
+    s_up=((2, 4, 2, 192, 384), BF),
+    s_down=((4, 2, 2, 96, 768), BF),
+    **{"r1_" + k: v for k, v in slots(2).items()},
+    **{"r2_" + k: v for k, v in slots(1).items()},
+    r3_sq=((3, 7, 48, 384), BF),
+    r3_up=((3, 192, 384), BF),
+    r3_down=((3, 96, 768), BF),
+    vbuf=((10, 16, 768), F32),
+    **ACTIVE,
+)
+SEMS = dict(load=20, swap=2, ag_s=(N_GROUPS, 19), ag_r=(N_GROUPS, 19), rs_s=(N_GROUPS, 10), rs_r=(N_GROUPS, 10), vs=6, vr=6, ends=4, endr=4)
+
+
+def layer_kernel(*refs):
+    r = Refs()
+    names = (
+        ["length", "tokens_in", "og_in", "gains_in", "shifts_in", "pool_in"]
+        + [f"shard{m}" for m in range(7)]
+        + ["up_in", "down_in", "out", "din", "vec", "o_sq", "o_up", "o_down"]
+        + list(BUFFERS)
+        + list(SEMS)
+    )
+    for name, ref in zip(names, refs):
+        setattr(r, name, ref)
+    alias_late(r)
+    me = Place()
+
+    shards = [r.shards.at[m] for m in range(7)]
+    pairs = [(getattr(r, f"shard{m}"), shards[m]) for m in range(7)]
+    pairs += [
+        (r.down_in, r.down.at[me.z, me.x, me.y, me.c]),
+        (r.up_in, r.up.at[me.y, me.c, me.z, me.x]),
+        (r.tokens_in, r.tokens),
+        (r.pool_in, r.pool),
+        (r.gains_in, r.gains),
+        (r.shifts_in, r.shifts),
+        (r.og_in, r.og),
+    ]
+    loads = [pltpu.make_async_copy(a, b, r.load.at[i]) for i, (a, b) in enumerate(pairs)]
+    for cp in loads:
+        cp.start()
+    greet(me)
+    weights = (r.sq, r.up, r.down)
+    gat = Gather(me, weights, r.ag_s, r.ag_r)
+    sca = Scatter(
+        me,
+        weights,
+        (r.s_sq, r.s_up, r.s_down),
+        (r.r1_sq, r.r1_up, r.r1_down),
+        (r.r2_sq, r.r2_up, r.r2_down),
+        (r.r3_sq, r.r3_up, r.r3_down),
+        r.rs_s,
+        r.rs_r,
+    )
+
+    for cp in loads[:9]:
+        cp.wait()
+    place_squares(me, shards, r.sq, r.act, r.swap.at[0], r.swap.at[1])
+    for g in range(N_GROUPS):
+        gat.start(g)
+    set_masks(r, r.length[0])
+    gat.step0(0)
+    gat.step0(1)
+    gat.step1(0)
+    gat.step0(2)
+    gat.step1(1)
+    gat.step0(3)
+    gat.step2(0)
+    gat.step1(2)
+    gat.step0(4)
+    gat.step2(1)
+    gat.step3(0)
+    gat.step1(3)
+    gat.step0(5)
+    gat.step2(2)
+    gat.step3(1)
+    gat.step4(0)
+    gat.step1(4)
+    gat.step0(6)
+    for cp in loads[9:]:
+        cp.wait()
+    gat.arrived(0)
+    project(r, 0, 1)
+    gat.step2(3)
+    gat.step3(2)
+    gat.step4(1)
+    gat.step1(5)
+    gat.step0(7)
+    gat.arrived(1)
+    project(r, 1, 3)
+    gat.step2(4)
+    gat.step3(3)
+    gat.step4(2)
+    gat.step1(6)
+    gat.arrived(2)
+    project_pool(r, 0)
+    project_pool(r, 1)
+
+    def ahead_a():
+        gat.step1(7)
+        gat.step2(5)
+
+    def ahead_b():
+        gat.step3(4)
+        gat.step4(3)
+
+    level_one(r, {2: ahead_a, 4: ahead_b})
+    gat.step2(6)
+    gat.step3(5)
+    gat.step4(4)
+    gat.arrived(3)
+    level_two(r)
+    gat.step2(7)
+    gat.step3(6)
+    gat.step4(5)
+    first_norm(r)
+    gat.step3(7)
+    gat.step4(6)
+    gat.arrived(4)
+    gat.arrived(5)
+    ffn_up(r)
+    gat.step4(7)
+    gat.arrived(6)
+    gat.arrived(7)
+    ffn_down_norm(r)
+    out = pltpu.make_async_copy(r.og, r.out, r.load.at[0])
+    out.start()
+    for g in range(N_GROUPS):
+        gat.sent(g)
+
+    for c in (1 - me.c, me.c):
+        back_down(r, c)
+        if c is not me.c:
+            sca.start(6)
+            sca.start(7)
+    sca.step1(6)
+    sca.step1(7)
+    back_first_norm(r)
+    grad_up(r)
+    sca.start(4)
+    sca.start(5)
+    sca.step2(6)
+    back_out(r)
+    sca.step1(4)
+    sca.step1(5)
+    sca.step2(7)
+
+    def two_a():
+        sca.step3(6)
+
+    def two_b():
+        sca.step3(7)
+
+    back_level_two(r, {2: two_a, 5: two_b})
+    sca.start(3)
+    sca.step2(4)
+    back_pool(r, 0)
+    sca.step1(3)
+    back_pool(r, 1)
+    sca.start(2)
+    sca.step2(5)
+    sca.step3(4)
+    total = VectorSum(me, r.vec, r.vbuf, r.vs, r.vr)
+    total.send(0)
+
+    def one_a():
+        sca.step1(2)
+        r.o_down[0:48] = sca.finish(6)
+        total.take(0)
+        total.send(1)
+
+    def one_b():
+        sca.step3(5)
+        r.o_down[48:96] = sca.finish(7)
+        total.take(1)
+        total.send(2)
+
+    def one_c():
+        sca.step2(3)
+        total.take(2)
+        total.send_z()
+
+    def one_d():
+        r.o_up[0:96] = sca.finish(4)
+        total.take_z()
+
+    back_level_one(r, {2: one_a, 4: one_b, 8: one_c, 10: one_d})
+    finish_projection(r, 1, r.dqkv[1])
+    finish_projection(r, 2, r.dqkv[2])
+    sca.start(1)
+    sca.step2(2)
+    sca.step3(3)
+    finish_projection(r, 0, r.dqkv[0])
+    sca.start(0)
+    sca.step1(1)
+    sca.step1(0)
+    r.dlow[...] = r.dr[...].astype(BF)
+    din = pltpu.make_async_copy(r.dlow, r.din, r.load.at[1])
+    din.start()
+    r.o_up[96:192] = sca.finish(5)
+
+    def end_swap(g, incoming=False):
+        _, lo, hi = GROUPS[g]
+        b = r.o_sq.at[lo:hi, 1 - me.c if incoming else me.c]
+        return rcopy(b, b, r.ends.at[g], r.endr.at[g], me.sibling())
+
+    def end(g):
+        _, lo, hi = GROUPS[g]
+        r.o_sq[lo:hi, me.c] = sca.finish(g)
+        end_swap(g).start()
+
+    sca.step3(2)
+    end(3)
+    sca.step2(1)
+    sca.step2(0)
+    end(2)
+    sca.step3(1)
+    sca.step3(0)
+    end(1)
+    end(0)
+    for g in range(N_GROUPS):
+        sca.sent(g)
+    for g in range(4):
+        end_swap(g).wait_send()
+        end_swap(g, True).wait_recv()
+    out.wait()
+    din.wait()
+
+
+def layer(length, tokens, og, gains, shifts, pool, squares, up, down):
+    vmem = pl.BlockSpec(memory_space=pltpu.VMEM)
+    hbm = pl.BlockSpec(memory_space=pl.ANY)
+    return pl.pallas_call(
+        layer_kernel,
+        out_shape=[
+            jax.ShapeDtypeStruct((512, 768), BF),
+            jax.ShapeDtypeStruct((512, 768), BF),
+            jax.ShapeDtypeStruct((16, 768), F32),
+            jax.ShapeDtypeStruct((7, 2, 48, 384), F32),
+            jax.ShapeDtypeStruct((192, 384), F32),
+            jax.ShapeDtypeStruct((96, 768), F32),
+        ],
+        in_specs=[pl.BlockSpec(memory_space=pltpu.SMEM)] + [hbm] * 14,
+        out_specs=[hbm] * 2 + [vmem] * 4,
+        scratch_shapes=[pltpu.VMEM(*s) for s in BUFFERS.values()]
+        + [pltpu.SemaphoreType.DMA(s if isinstance(s, tuple) else (s,)) for s in SEMS.values()],
+        compiler_params=pltpu.CompilerParams(
+            collective_id=0, has_side_effects=True, vmem_limit_bytes=VMEM_LIMIT
+        ),
+    )(length, tokens, og, gains, shifts, pool, *squares, up, down)
+
+
+VMEM_LIMIT = 63 * 2**20
+
+
+def ending_kernel(*refs):
+    act, din, vec, sq, up, down, o_act, o_din = refs[:8]
+    o_sq = refs[8:15]
+    o_up, o_down, o_gain, o_shift, o_pool, turned = refs[15:]
+    o_act[...] = act[...]
+    o_din[...] = din[...]
+    o_up[...] = up[...]
+    o_down[...] = down[...]
+    core = lax.rem(lax.axis_index("dp"), 2)
+    mine = pl.ds(pl.multiple_of(core * 192, 8), 192)
+    for m in range(7):
+        turned[...] = jnp.transpose(sq[m].reshape(96, 384))
+        o_sq[m][...] = turned[mine, :]
+    o_gain[...] = vec[GAIN : GAIN + 2]
+    o_shift[...] = vec[SHIFT : SHIFT + 2]
+    for t in range(5):
+        o_pool[t] = vec[POOL + 2 * t : POOL + 2 * t + 2]
+
+
+def ending(act, din, vec, sq, up, down):
+    vmem = pl.BlockSpec(memory_space=pltpu.VMEM)
+    shapes = [((512, 768), BF)] * 2 + [((192, 96), F32)] * 7 + [((192, 384), F32), ((96, 768), F32)]
+    shapes += [((2, 768), F32)] * 2 + [((5, 2, 768), F32)]
+    return pl.pallas_call(
+        ending_kernel,
+        out_shape=[jax.ShapeDtypeStruct(*s) for s in shapes],
+        in_specs=[vmem] * 6,
+        out_specs=[vmem] * len(shapes),
+        scratch_shapes=[pltpu.VMEM((384, 96), F32)],
+        compiler_params=pltpu.CompilerParams(vmem_limit_bytes=32 * 2**20),
+    )(act, din, vec, sq, up, down)
+
+
+def local_kernels(
+    tokens,
+    doc_lengths,
+    w_query,
+    w_key,
+    w_value,
+    w_query2,
+    w_key2,
+    w_value2,
+    w_out,
+    w_up,
+    w_down,
+    norm_gains,
+    norm_shifts,
+    pool_kernels,
+    out_grad,
+):
+    squares = (w_query, w_key, w_value, w_key2, w_value2, w_query2, w_out)
+    ends = layer(
+        doc_lengths,
+        tokens,
+        out_grad,
+        norm_gains,
+        norm_shifts,
+        pool_kernels.transpose(1, 0, 2),
+        squares,
+        w_up,
+        w_down.T,
+    )
+    act, din, g_q, g_k, g_v, g_k2, g_v2, g_q2, g_out, g_up, g_down, gain, shift, pools = ending(*ends)
+    return (
+        act,
+        din,
+        g_q,
+        g_k,
+        g_v,
+        g_q2,
+        g_k2,
+        g_v2,
+        g_out,
+        g_up,
+        g_down.T,
+        gain,
+        shift,
+        pools.transpose(1, 0, 2),
     )
 
 
@@ -405,8 +1406,9 @@
 
 
 def solution(mesh):
+    fits = mesh.shape["dp"] == 4 and mesh.shape["fsdp"] == 8
     return jax.shard_map(
-        local,
+        local_kernels if fits else local,
         mesh=mesh,
         in_specs=(
             P(("dp", "fsdp"), None),

time: 1330 us -> 210 us (0.16)
  waiting for transfers between devices: 691 us -> 0 us
  blocking collectives: 219 us -> 0 us
  matrix products: 209 us -> 0 us
  Pallas kernels: 0 us -> 202 us
  local copies, waits for them, and re-layouts: 131 us -> 6.2 us
  other arithmetic: 48.3 us -> 0 us
  between operations: 16.8 us -> 1.41 us
    reduce_scatter x10 -> x0, waiting for transfers between devices: 404 us -> none  [the longest x1 97.4 us: reduce_columns_first(): lax.psum_scatter(grads_all[8].astype(jnp.bfloat16), 'fsdp', scatter_dimen...]
    dot_general x111 -> x0, matrix products: 209 us -> none  [the longest x9 33.7 us: inner_rows(): lax.dot_general(left_mat, right_mat, (((0,), (0,)), ((), ())), preferred_...]
    pallas_call x0 -> x2, Pallas kernels: none -> 202 us  [the longest x1 200 us: layer(): pl.pallas_call(layer_kernel, out_shape=[jax.ShapeDtypeStruct((512, 768),...]
    unnamed x37 -> x0, waiting for transfers between devices: 190 us -> none
    all_gather x7 -> x0, blocking collectives: 175 us -> none  [the longest x1 26.2 us: gather_first(): lax.all_gather(shards[4], 'fsdp', axis=1, tiled=True)]
    all_gather x11 -> x0, waiting for transfers between devices: 97.5 us -> none  [the longest x1 32.8 us: gather_first(): lax.all_gather(column_parts[7], 'dp', axis=0, tiled=True)]
    unnamed x233 -> x12, local copies, waits for them, and re-layouts: 63.8 us -> 6.2 us
    psum x1 -> x0, blocking collectives: 43.2 us -> none  [local(): lax.psum((gain_stack, shift_stack, pool_stack), ('dp', 'fsdp'))]
  transfers between devices with their start and end apart: 29 -> 0, of which waited for: 19 -> 0; matrix products, arithmetic and copies ran while one was open for 26% -> 0% of each run, Pallas kernels for 0% -> 0%
where the time goes in v2:
time: 210 us; the launch traced here: 209 us
  Pallas kernels  202 us (96%)
  local copies, waits for them, and re-layouts  6.2 us (3%)
    pallas_call x1, Pallas kernels, layer(): pl.pallas_call(layer_kernel, out_shape=[jax.ShapeDtypeStruct((512, 768),...  200 us
    unnamed x12, local copies, waits for them, and re-layouts  6.2 us

profile of v2, /device:TPU:1, one launch (start us, length us, event | category | flops | bytes accessed | tf_op | source)
XLA Modules:
  0.0 209.2 jit_solution(17443197536742224032)
XLA Ops:
  1.3 199.5 %shard_map.254 = (bf16[512,768]{1,0:T(8,128)(2,1)}, bf16[512,768]{1,0:T(8,128)(2,1)}, f32[16,768]{1,0:T(8,128)}, f32[7,2,48,384]{3,2,1,0:T(8,128)}, f32[192,384]{1,0:T(8,128)}, /*index=5*/f32[96,768]{1,0:T(8,128)}) custom-call(s32[1]{0:T(128)S(6)} %copy.29.refs_0_, bf16[512,768]{1,0:T(8,128)(2,1)} %refs_1_.1, bf16[512,768]{1,0:T(8,128)(2,1)} %refs_2_.1, ...), custom_call_target="tpu_custom_call" | custom-call | tf_op jit(solution)/shard_map/pallas_call | solution.py:1145
  200.8 0.0 copy-start
  200.8 1.2 copy-done
  202.0 0.0 copy-start.1
  202.0 1.1 copy-done.1
  203.2 0.0 copy-start.2
  203.2 1.1 copy-done.2
  204.3 0.0 copy-start.3
  204.3 1.0 copy-done.3
  205.3 0.0 copy-start.4
  205.3 1.0 copy-done.4
  206.2 0.0 copy-start.5
  206.2 0.8 copy-done.5
  207.0 2.1 shard_map.255
Async XLA Ops:
  200.8 1.2 copy-start
  202.0 1.1 copy-start.1
  203.2 1.1 copy-start.2
  204.3 1.0 copy-start.3
  205.3 1.0 copy-start.4
  206.2 0.8 copy-start.5

commit v3 on v2

--- a/solution.py
+++ b/solution.py
@@ -258,9 +258,11 @@
     ("s", 5, 7),
     ("u", 0, 96),
     ("u", 96, 192),
-    ("d", 0, 48),
-    ("d", 48, 96),
+    ("d", 0, 256),
+    ("d", 256, 512),
+    ("d", 512, 768),
 )
+PLANE = 8
 N_GROUPS = len(GROUPS)
 SQ = (7, 4, 2, 2, 48, 768)
 UP = (2, 2, 4, 2, 192, 384)
@@ -293,7 +295,7 @@
         return lax.rem(self.z + k, 4)
 
     def everyone(self):
-        return [self.sibling(), self.dev(self.p1), self.dev(self.p2)] + [
+        return [self.sibling(), self.dev(self.p1), self.dev(self.p2), self.dev(self.diag)] + [
             self.dev(self.own, z=self.peer(k)) for k in (1, 2, 3)
         ]
 
@@ -302,7 +304,7 @@
     bar = pltpu.get_barrier_semaphore()
     for d in me.everyone():
         pl.semaphore_signal(bar, inc=1, device_id=d, device_id_type=MESH)
-    pl.semaphore_wait(bar, 6)
+    pl.semaphore_wait(bar, 7)
 
 
 def square_lanes(y):
@@ -317,7 +319,12 @@
         return sq.at[lo:hi, z, x, c, :, square_lanes(y)]
     if kind == "u":
         return up.at[y, c, z, x, lo:hi]
-    return down.at[z, x, y, c, lo:hi]
+    return down.at[z, x, y, c, :, lo:hi]
+
+
+def plane(down, g, c, z):
+    _, lo, hi = GROUPS[g]
+    return down.at[z, :, :, c, :, lo:hi]
 
 
 def rcopy(src, dst, ssem, rsem, dev):
@@ -397,9 +404,10 @@
 
 
 class Scatter:
-    def __init__(self, me, refs, sib, r1, r2, r3, ssem, rsem):
+    def __init__(self, me, refs, sib, r1, r2, r3, rp, ssem, rsem):
         self.me, self.refs, self.sib = me, refs, sib
         self.r1, self.r2, self.r3 = r1, r2, r3
+        self.pz, self.p2, self.p1 = rp
         self.ssem, self.rsem = ssem, rsem
 
     def sib_view(self, g, xy, z=slice(None)):
@@ -410,19 +418,40 @@
             return sq.at[lo:hi, z, x, :, square_lanes(y)]
         if kind == "u":
             return up.at[y, z, x, lo:hi]
-        return down.at[z, x, y, lo:hi]
+        return down.at[z, x, y, :, lo:hi]
+
+    def plane_of(self, g, c, z):
+        return plane(self.refs[2], g, c, z)
+
+    def sib_plane(self, g, z):
+        _, lo, hi = GROUPS[g]
+        return self.sib[2].at[z, :, :, :, lo:hi]
 
     def slot(self, bufs, g, i):
         kind, lo, hi = GROUPS[g]
         if kind == "s":
             return bufs[0].at[i, lo:hi]
         buf = bufs[1 if kind == "u" else 2]
+        if kind == "d":
+            return buf.at[i, :, :, lo:hi] if len(buf.shape) == 4 else buf.at[i, :, lo:hi]
         return buf.at[i, :, lo:hi] if len(buf.shape) == 4 else buf.at[i, lo:hi]
 
     def copy(self, g, i):
         me = self.me
         c = me.c
         ss, rs = self.ssem.at[g, i], self.rsem.at[g, i]
+        if g == PLANE:
+            if i < 4:
+                z = me.peer(i + 1)
+                return rcopy(self.plane_of(g, 1 - c, z), self.sib_plane(g, z), ss, rs, me.sibling())
+            if i < 7:
+                k = i - 3
+                src = self.plane_of(g, c, me.peer(k))
+                return rcopy(src, self.pz.at[k - 1], ss, rs, me.dev(me.own, z=me.peer(k)))
+            if i < 9:
+                src = blocks(self.refs, g, (me.diag, me.p2)[i - 7], c, me.z)
+                return rcopy(src, self.p2.at[i - 7], ss, rs, me.dev(me.p2))
+            return rcopy(blocks(self.refs, g, me.p1, c, me.z), self.p1, ss, rs, me.dev(me.p1))
         if i < 4:
             what = (me.p1, me.diag, me.p2, me.own)[i]
             return rcopy(blocks(self.refs, g, what, 1 - c), self.sib_view(g, what), ss, rs, me.sibling())
@@ -453,6 +482,13 @@
 
     def step1(self, g):
         me = self.me
+        if g == PLANE:
+            for k in (1, 2, 3):
+                z = me.peer(k)
+                self.got(g, k - 1)
+                self.add(self.plane_of(g, me.c, z), self.sib_plane(g, z))
+                self.go(g, 3 + k)
+            return
         for i, what, out in ((1, me.diag, 4), (0, me.p2, 5)):
             self.got(g, i)
             self.add(blocks(self.refs, g, what, me.c), self.sib_view(g, what))
@@ -460,6 +496,13 @@
 
     def step2(self, g):
         me = self.me
+        if g == PLANE:
+            for i in (3, 4, 5, 6):
+                self.got(g, i)
+            here = self.plane_of(g, me.c, me.z)
+            self.add(here, self.sib_plane(g, me.z), *[self.pz.at[k] for k in range(3)])
+            self.go(g, 7, 8)
+            return
         self.got(g, 2)
         self.got(g, 4)
         here = blocks(self.refs, g, me.p1, me.c)
@@ -468,6 +511,11 @@
 
     def step3(self, g):
         me = self.me
+        if g == PLANE:
+            self.got(g, 7)
+            self.add(blocks(self.refs, g, me.p1, me.c, me.z), self.p2.at[0])
+            self.go(g, 9)
+            return
         self.got(g, 3)
         self.got(g, 5)
         self.got(g, 6)
@@ -478,6 +526,10 @@
     def finish(self, g):
         me = self.me
         total = blocks(self.refs, g, me.own, me.c, me.z)[...].astype(F32)
+        if g == PLANE:
+            self.got(g, 8)
+            self.got(g, 9)
+            return total + self.p2[1].astype(F32) + self.p1[...].astype(F32)
         for k in (1, 2, 3):
             self.got(g, 6 + k)
             total = total + self.slot(self.r3, g, k - 1)[...].astype(F32)
@@ -491,37 +543,50 @@
 class VectorSum:
     def __init__(self, me, vec, buf, ssem, rsem):
         self.me, self.vec, self.buf, self.ssem, self.rsem = me, vec, buf, ssem, rsem
-        self.hops = [me.sibling(), me.dev((1 - me.x, me.y)), me.dev((me.x, 1 - me.y))]
-
-    def hop(self, i):
+
+    def copy(self, i, incoming=False):
+        me = self.me
+        if i < 3:
+            z = lax.rem(me.z + 3 - i, 4) if incoming else me.z
+            b, d = self.buf.at[z], me.dev(me.own, z=me.peer(i + 1))
+        elif i == 3:
+            return rcopy(self.buf.at[4], self.buf.at[5], self.ssem.at[i], self.rsem.at[i], me.sibling())
+        else:
+            x, y = ((1 - me.x, me.y), (me.x, 1 - me.y), me.diag)[i - 4]
+            fx, fy = (x, y) if incoming else me.own
+            b, d = self.buf.at[6 + fx + 2 * fy], me.dev((x, y))
+        return rcopy(b, b, self.ssem.at[i], self.rsem.at[i], d)
+
+    def send(self, first, last):
+        for i in range(first, last):
+            self.copy(i).start()
+
+    def got(self, first, last):
+        for i in range(first, last):
+            self.copy(i, True).wait_recv()
+
+    def send_z(self):
+        self.buf[self.me.z] = self.vec[...]
+        self.send(0, 3)
+
+    def send_core(self):
+        self.got(0, 3)
         b = self.buf
-        return rcopy(b.at[i], b.at[3 + i], self.ssem.at[i], self.rsem.at[i], self.hops[i])
-
-    def send(self, i):
-        self.buf[i] = self.vec[...]
-        self.hop(i).start()
-
-    def take(self, i):
-        self.hop(i).wait()
-        self.vec[...] = self.vec[...] + self.buf[3 + i]
-
-    def zcopy(self, k, incoming):
-        me = self.me
-        b = self.buf.at[6 + (lax.rem(me.z + 4 - k, 4) if incoming else me.z)]
-        return rcopy(b, b, self.ssem.at[2 + k], self.rsem.at[2 + k], me.dev(me.own, z=me.peer(k)))
-
-    def send_z(self):
-        self.buf[6 + self.me.z] = self.vec[...]
-        for k in (1, 2, 3):
-            self.zcopy(k, False).start()
-
-    def take_z(self):
-        for k in (1, 2, 3):
-            self.zcopy(k, True).wait_recv()
-        for k in (1, 2, 3):
-            self.zcopy(k, False).wait_send()
+        b[4] = (b[0] + b[1]) + (b[2] + b[3])
+        self.send(3, 4)
+
+    def send_beside(self):
+        self.got(3, 4)
+        b = self.buf
+        b[6 + self.me.x + 2 * self.me.y] = b[4] + b[5]
+        self.send(4, 7)
+
+    def take(self):
+        self.got(4, 7)
         b = self.buf
         self.vec[...] = (b[6] + b[7]) + (b[8] + b[9])
+        for i in range(7):
+            self.copy(i).wait_send()
 
 
 def place_squares(me, shards, sq, room, ssem, rsem):
@@ -559,8 +624,8 @@
     return jnp.concatenate([left, right], axis=1)
 
 
-def weight_down(r, y, c):
-    return r.down[:, :, y, c].reshape(768, 768)
+def weight_down(r, y, c, lo, hi):
+    return r.down[:, :, y, c, :, lo:hi].reshape(768, hi - lo)
 
 
 def set_masks(r, length):
@@ -712,15 +777,18 @@
             r.gd[j, rows] = slope.astype(BF)
 
 
-def ffn_down_norm(r):
+def ffn_down(r, lo, hi):
     @pl.loop(0, 2)
     def _(i):
         rows = pl.ds(pl.multiple_of(256 * i, 256), 256)
-        total = dg(r.act[0, rows], weight_down(r, 0, 0), 1, 1)
-        for j in range(1, 4):
-            total = total + dg(r.act[j, rows], weight_down(r, j // 2, j % 2), 1, 1)
+        total = r.acc[rows] if lo else None
+        for j in range(4):
+            term = dg(r.act[j, rows, lo:hi], weight_down(r, j // 2, j % 2, lo, hi), 1, 1)
+            total = term if total is None else total + term
         r.acc[rows] = total
 
+
+def second_norm(r):
     r.vec[...] = jnp.zeros_like(r.vec)
 
     @pl.loop(0, 4)
@@ -737,15 +805,15 @@
         r.dlow[rows] = d.astype(BF)
 
 
-def back_down(r, c):
+def back_down(r, c, lo, hi):
     @pl.loop(0, 2)
     def _(y):
         j = y * 2 + c
-        t = dg(r.dlow[...], weight_down(r, y, c), 1, 0)
-        r.gd[j] = (r.gd[j].astype(F32) * t).astype(BF)
+        t = dg(r.dlow[...], weight_down(r, y, c, lo, hi), 1, 0)
+        r.gd[j, :, lo:hi] = (r.gd[j, :, lo:hi].astype(F32) * t).astype(BF)
         for i in range(2):
-            g = dg(r.dlow[:, 384 * i : 384 * i + 384], r.act[j], 0, 0).astype(BF)
-            r.down[2 * i : 2 * i + 2, :, y, c] = g.reshape(2, 2, 96, 768)
+            g = dg(r.dlow[:, 384 * i : 384 * i + 384], r.act[j, :, lo:hi], 0, 0).astype(BF)
+            r.down[2 * i : 2 * i + 2, :, y, c, :, lo:hi] = g.reshape(2, 2, 96, hi - lo)
 
 
 def back_first_norm(r):
@@ -895,7 +963,7 @@
     return dict(
         sq=((n, 7, 4, 48, 384), BF),
         up=((n, 4, 192, 384), BF),
-        down=((n, 4, 96, 768), BF),
+        down=((n, 4, 96, 512), BF),
     )
 
 
@@ -915,12 +983,19 @@
     **{"r1_" + k: v for k, v in slots(2).items()},
     **{"r2_" + k: v for k, v in slots(1).items()},
     r3_sq=((3, 7, 48, 384), BF),
+    pz=((3, 2, 2, 96, 256), BF),
+    p2=((2, 96, 256), BF),
+    p1=((96, 256), BF),
+    b_sq=((7, 2, 48, 384), F32),
+    b_up=((192, 384), F32),
+    b_down=((96, 768), F32),
+    vec=((16, 768), F32),
     r3_up=((3, 192, 384), BF),
-    r3_down=((3, 96, 768), BF),
+    r3_down=((3, 96, 512), BF),
     vbuf=((10, 16, 768), F32),
     **ACTIVE,
 )
-SEMS = dict(load=20, swap=2, ag_s=(N_GROUPS, 19), ag_r=(N_GROUPS, 19), rs_s=(N_GROUPS, 10), rs_r=(N_GROUPS, 10), vs=6, vr=6, ends=4, endr=4)
+SEMS = dict(load=20, swap=2, ag_s=(N_GROUPS, 19), ag_r=(N_GROUPS, 19), rs_s=(N_GROUPS, 10), rs_r=(N_GROUPS, 10), vs=7, vr=7, ends=4, endr=4, outs=13)
 
 
 def layer_kernel(*refs):
@@ -928,7 +1003,7 @@
     names = (
         ["length", "tokens_in", "og_in", "gains_in", "shifts_in", "pool_in"]
         + [f"shard{m}" for m in range(7)]
-        + ["up_in", "down_in", "out", "din", "vec", "o_sq", "o_up", "o_down"]
+        + ["up_in", "down_in", "out", "din", "o_vec", "o_sq", "o_up", "o_down"]
         + list(BUFFERS)
         + list(SEMS)
     )
@@ -961,22 +1036,31 @@
         (r.r1_sq, r.r1_up, r.r1_down),
         (r.r2_sq, r.r2_up, r.r2_down),
         (r.r3_sq, r.r3_up, r.r3_down),
+        (r.pz, r.p2, r.p1),
         r.rs_s,
         r.rs_r,
     )
 
-    for cp in loads[:9]:
+    loads[7].wait()
+    gat.start(6)
+    for cp in loads[:7]:
         cp.wait()
     place_squares(me, shards, r.sq, r.act, r.swap.at[0], r.swap.at[1])
-    for g in range(N_GROUPS):
+    for g in range(4):
+        gat.start(g)
+    gat.step0(6)
+    loads[8].wait()
+    for g in (4, 5, 7, 8):
         gat.start(g)
     set_masks(r, r.length[0])
+    gat.step1(6)
     gat.step0(0)
     gat.step0(1)
     gat.step1(0)
     gat.step0(2)
     gat.step1(1)
     gat.step0(3)
+    gat.step2(6)
     gat.step2(0)
     gat.step1(2)
     gat.step0(4)
@@ -988,7 +1072,6 @@
     gat.step3(1)
     gat.step4(0)
     gat.step1(4)
-    gat.step0(6)
     for cp in loads[9:]:
         cp.wait()
     gat.arrived(0)
@@ -998,149 +1081,164 @@
     gat.step4(1)
     gat.step1(5)
     gat.step0(7)
+    gat.step0(8)
+    gat.step1(7)
     gat.arrived(1)
     project(r, 1, 3)
     gat.step2(4)
     gat.step3(3)
     gat.step4(2)
-    gat.step1(6)
+    gat.step1(8)
     gat.arrived(2)
     project_pool(r, 0)
     project_pool(r, 1)
 
-    def ahead_a():
-        gat.step1(7)
-        gat.step2(5)
-
     def ahead_b():
         gat.step3(4)
         gat.step4(3)
 
-    level_one(r, {2: ahead_a, 4: ahead_b})
-    gat.step2(6)
+    level_one(r, {2: lambda: gat.step2(5), 4: ahead_b})
+    gat.step2(7)
     gat.step3(5)
+    gat.step3(6)
+    gat.step4(6)
     gat.step4(4)
     gat.arrived(3)
     level_two(r)
-    gat.step2(7)
-    gat.step3(6)
+    gat.step2(8)
+    gat.step3(7)
     gat.step4(5)
     first_norm(r)
-    gat.step3(7)
-    gat.step4(6)
+    gat.step3(8)
+    gat.step4(7)
     gat.arrived(4)
     gat.arrived(5)
     ffn_up(r)
-    gat.step4(7)
+    gat.step4(8)
     gat.arrived(6)
     gat.arrived(7)
-    ffn_down_norm(r)
+    ffn_down(r, 0, 512)
+    gat.arrived(8)
+    ffn_down(r, 512, 768)
+    second_norm(r)
     out = pltpu.make_async_copy(r.og, r.out, r.load.at[0])
     out.start()
     for g in range(N_GROUPS):
         gat.sent(g)
 
-    for c in (1 - me.c, me.c):
-        back_down(r, c)
-        if c is not me.c:
-            sca.start(6)
-            sca.start(7)
-    sca.step1(6)
-    sca.step1(7)
+    def flush(src, dst, i):
+        cp = pltpu.make_async_copy(src, dst, r.outs.at[i])
+        cp.start()
+        pending.append(cp)
+
+    pending = []
+
+    def give(g):
+        kind, lo, hi = GROUPS[g]
+        if kind == "u":
+            r.b_up[lo:hi] = sca.finish(g)
+            flush(r.b_up.at[lo:hi], r.o_up.at[lo:hi], g)
+        else:
+            r.b_down[:, lo:hi] = sca.finish(g)
+            flush(r.b_down.at[:, lo:hi], r.o_down.at[:, lo:hi], g)
+
+    def end_swap(g, incoming=False):
+        _, lo, hi = GROUPS[g]
+        b = r.b_sq.at[lo:hi, 1 - me.c if incoming else me.c]
+        return rcopy(b, b, r.ends.at[g], r.endr.at[g], me.sibling())
+
+    def end(g):
+        _, lo, hi = GROUPS[g]
+        r.b_sq[lo:hi, me.c] = sca.finish(g)
+        end_swap(g).start()
+        flush(r.b_sq.at[lo:hi, me.c], r.o_sq.at[lo:hi, me.c], g)
+
+    def close(g):
+        _, lo, hi = GROUPS[g]
+        end_swap(g, True).wait_recv()
+        flush(r.b_sq.at[lo:hi, 1 - me.c], r.o_sq.at[lo:hi, 1 - me.c], N_GROUPS + g)
+
+    for g in (6, 8, 7):
+        _, lo, hi = GROUPS[g]
+        back_down(r, 1 - me.c, lo, hi)
+        sca.start(g)
+        back_down(r, me.c, lo, hi)
+        sca.step1(g)
+    sca.step2(6)
     back_first_norm(r)
     grad_up(r)
     sca.start(4)
     sca.start(5)
-    sca.step2(6)
+    sca.step2(7)
+    sca.step3(6)
     back_out(r)
     sca.step1(4)
     sca.step1(5)
-    sca.step2(7)
-
-    def two_a():
-        sca.step3(6)
-
-    def two_b():
-        sca.step3(7)
-
-    back_level_two(r, {2: two_a, 5: two_b})
+    back_level_two(r)
     sca.start(3)
-    sca.step2(4)
+    sca.step3(7)
     back_pool(r, 0)
     sca.step1(3)
+    sca.step2(8)
     back_pool(r, 1)
     sca.start(2)
-    sca.step2(5)
-    sca.step3(4)
     total = VectorSum(me, r.vec, r.vbuf, r.vs, r.vr)
-    total.send(0)
-
-    def one_a():
-        sca.step1(2)
-        r.o_down[0:48] = sca.finish(6)
-        total.take(0)
-        total.send(1)
-
-    def one_b():
-        sca.step3(5)
-        r.o_down[48:96] = sca.finish(7)
-        total.take(1)
-        total.send(2)
-
-    def one_c():
-        sca.step2(3)
-        total.take(2)
-        total.send_z()
-
-    def one_d():
-        r.o_up[0:96] = sca.finish(4)
-        total.take_z()
-
-    back_level_one(r, {2: one_a, 4: one_b, 8: one_c, 10: one_d})
+    total.send_z()
+
+    back_level_one(
+        r,
+        {
+            2: lambda: sca.step1(2),
+            3: lambda: sca.step2(4),
+            7: total.send_core,
+            8: lambda: sca.step2(5),
+            9: total.send_beside,
+            11: lambda: sca.step3(4),
+        },
+    )
     finish_projection(r, 1, r.dqkv[1])
     finish_projection(r, 2, r.dqkv[2])
     sca.start(1)
-    sca.step2(2)
-    sca.step3(3)
+    sca.step2(3)
+    sca.step3(5)
     finish_projection(r, 0, r.dqkv[0])
     sca.start(0)
     sca.step1(1)
     sca.step1(0)
+    sca.step3(8)
     r.dlow[...] = r.dr[...].astype(BF)
     din = pltpu.make_async_copy(r.dlow, r.din, r.load.at[1])
     din.start()
-    r.o_up[96:192] = sca.finish(5)
-
-    def end_swap(g, incoming=False):
-        _, lo, hi = GROUPS[g]
-        b = r.o_sq.at[lo:hi, 1 - me.c if incoming else me.c]
-        return rcopy(b, b, r.ends.at[g], r.endr.at[g], me.sibling())
-
-    def end(g):
-        _, lo, hi = GROUPS[g]
-        r.o_sq[lo:hi, me.c] = sca.finish(g)
-        end_swap(g).start()
-
+    sca.step2(2)
+    sca.step3(3)
+    for g in (6, 7, 4, 5):
+        give(g)
     sca.step3(2)
-    end(3)
     sca.step2(1)
     sca.step2(0)
-    end(2)
+    give(8)
+    end(3)
     sca.step3(1)
     sca.step3(0)
+    end(2)
+    close(3)
+    close(2)
+    total.take()
+    vec_out = pltpu.make_async_copy(r.vec, r.o_vec, r.load.at[2])
+    vec_out.start()
     end(1)
     end(0)
     for g in range(N_GROUPS):
         sca.sent(g)
+    close(1)
+    close(0)
     for g in range(4):
         end_swap(g).wait_send()
-        end_swap(g, True).wait_recv()
-    out.wait()
-    din.wait()
+    for cp in [*pending, out, din, vec_out]:
+        cp.wait()
 
 
 def layer(length, tokens, og, gains, shifts, pool, squares, up, down):
-    vmem = pl.BlockSpec(memory_space=pltpu.VMEM)
     hbm = pl.BlockSpec(memory_space=pl.ANY)
     return pl.pallas_call(
         layer_kernel,
@@ -1153,7 +1251,7 @@
             jax.ShapeDtypeStruct((96, 768), F32),
         ],
         in_specs=[pl.BlockSpec(memory_space=pltpu.SMEM)] + [hbm] * 14,
-        out_specs=[hbm] * 2 + [vmem] * 4,
+        out_specs=[hbm] * 6,
         scratch_shapes=[pltpu.VMEM(*s) for s in BUFFERS.values()]
         + [pltpu.SemaphoreType.DMA(s if isinstance(s, tuple) else (s,)) for s in SEMS.values()],
         compiler_params=pltpu.CompilerParams(
@@ -1166,36 +1264,47 @@
 
 
 def ending_kernel(*refs):
-    act, din, vec, sq, up, down, o_act, o_din = refs[:8]
+    o_act, o_din, o_up, o_down = refs[6], refs[7], refs[15], refs[16]
     o_sq = refs[8:15]
-    o_up, o_down, o_gain, o_shift, o_pool, turned = refs[15:]
-    o_act[...] = act[...]
-    o_din[...] = din[...]
-    o_up[...] = up[...]
-    o_down[...] = down[...]
+    o_gain, o_shift, o_pool, vec, sq, turned, sem = refs[17:]
+    copies = [
+        pltpu.make_async_copy(a, b, sem.at[i])
+        for i, (a, b) in enumerate(zip(refs[:6], (o_act, o_din, vec, sq, o_up, o_down)))
+    ]
+    for i in (3, 2, 0, 1, 4, 5):
+        copies[i].start()
     core = lax.rem(lax.axis_index("dp"), 2)
     mine = pl.ds(pl.multiple_of(core * 192, 8), 192)
+    copies[3].wait()
     for m in range(7):
         turned[...] = jnp.transpose(sq[m].reshape(96, 384))
         o_sq[m][...] = turned[mine, :]
+    copies[2].wait()
     o_gain[...] = vec[GAIN : GAIN + 2]
     o_shift[...] = vec[SHIFT : SHIFT + 2]
     for t in range(5):
         o_pool[t] = vec[POOL + 2 * t : POOL + 2 * t + 2]
-
-
-def ending(act, din, vec, sq, up, down):
+    for i in (0, 1, 4, 5):
+        copies[i].wait()
+
+
+def ending(*parts):
     vmem = pl.BlockSpec(memory_space=pltpu.VMEM)
     shapes = [((512, 768), BF)] * 2 + [((192, 96), F32)] * 7 + [((192, 384), F32), ((96, 768), F32)]
     shapes += [((2, 768), F32)] * 2 + [((5, 2, 768), F32)]
     return pl.pallas_call(
         ending_kernel,
         out_shape=[jax.ShapeDtypeStruct(*s) for s in shapes],
-        in_specs=[vmem] * 6,
+        in_specs=[pl.BlockSpec(memory_space=pl.ANY)] * 6,
         out_specs=[vmem] * len(shapes),
-        scratch_shapes=[pltpu.VMEM((384, 96), F32)],
-        compiler_params=pltpu.CompilerParams(vmem_limit_bytes=32 * 2**20),
-    )(act, din, vec, sq, up, down)
+        scratch_shapes=[
+            pltpu.VMEM((16, 768), F32),
+            pltpu.VMEM((7, 2, 48, 384), F32),
+            pltpu.VMEM((384, 96), F32),
+            pltpu.SemaphoreType.DMA((6,)),
+        ],
+        compiler_params=pltpu.CompilerParams(vmem_limit_bytes=VMEM_LIMIT),
+    )(*parts)
 
 
 def local_kernels(

time: 210 us -> 186 us (0.89)
  Pallas kernels: 202 us -> 185 us
  local copies, waits for them, and re-layouts: 6.2 us -> 0 us
    pallas_call x1, Pallas kernels: 200 us -> 181 us  [layer(): pl.pallas_call(layer_kernel, out_shape=[jax.ShapeDtypeStruct((512, 768),...]
    unnamed x12 -> x0, local copies, waits for them, and re-layouts: 6.2 us -> none
where the time goes in v3:
time: 186 us
  Pallas kernels  185 us (99%)
    pallas_call x1, Pallas kernels, layer(): pl.pallas_call(layer_kernel, out_shape=[jax.ShapeDtypeStruct((512, 768),...  181 us

profile of v3, /device:TPU:1, one launch (start us, length us, event | category | flops | bytes accessed | tf_op | source)
XLA Modules:
  0.0 186.2 jit_solution(13338054365741979198)
XLA Ops:
  1.3 181.2 %shard_map.254 = (bf16[512,768]{1,0:T(8,128)(2,1)}, bf16[512,768]{1,0:T(8,128)(2,1)}, f32[16,768]{1,0:T(8,128)}, f32[7,2,48,384]{3,2,1,0:T(8,128)}, f32[192,384]{1,0:T(8,128)}, /*index=5*/f32[96,768]{1,0:T(8,128)}) custom-call(s32[1]{0:T(128)S(6)} %copy.29.refs_0_, bf16[512,768]{1,0:T(8,128)(2,1)} %refs_1_.1, bf16[512,768]{1,0:T(8,128)(2,1)} %refs_2_.1, ...), custom_call_target="tpu_custom_call" | custom-call | tf_op jit(solution)/shard_map/pallas_call | solution.py:1243
  182.5 3.5 %shard_map.255 = (bf16[512,768]{1,0:T(8,128)(2,1)}, bf16[512,768]{1,0:T(8,128)(2,1)}, f32[192,96]{1,0:T(8,128)}, f32[192,96]{1,0:T(8,128)}, f32[192,96]{1,0:T(8,...) custom-call(bf16[512,768]{1,0:T(8,128)(2,1)} %get-tuple-element.34.r, ...), custom_call_target="tpu_custom_call" | custom-call | tf_op jit(solution)/shard_map/pallas_call | solution.py:1295

commit v4 on v3

--- a/solution.py
+++ b/solution.py
@@ -253,7 +253,7 @@
 
 GROUPS = (
     ("s", 0, 1),
-    ("s", 1, 3),
+    ("s", 1, 2),
     ("s", 3, 5),
     ("s", 5, 7),
     ("u", 0, 96),
@@ -261,7 +261,9 @@
     ("d", 0, 256),
     ("d", 256, 512),
     ("d", 512, 768),
+    ("s", 2, 3),
 )
+SQUARES = (0, 1, 2, 3, 9)
 PLANE = 8
 N_GROUPS = len(GROUPS)
 SQ = (7, 4, 2, 2, 48, 768)
@@ -349,12 +351,15 @@
         if i < 6:
             k = i - 2
             z = lax.rem(me.z + 4 - k, 4) if incoming else me.z
-            b = blocks(self.refs, g, me.own, c, z)
+            b = plane(self.refs[2], g, c, z) if g == PLANE else blocks(self.refs, g, me.own, c, z)
             return rcopy(b, b, ss, rs, me.dev(me.own, z=me.peer(k)))
         if i < 10:
             cc = 1 - c if incoming else c
             what = ((me.own, me.own), (me.p1, me.p2), (me.p2, me.p1), (me.diag, me.diag))[i - 6][side]
-            b = blocks(self.refs, g, what, cc)
+            if g == PLANE:
+                b = plane(self.refs[2], g, cc, lax.rem(me.z + 4 - (i - 6), 4))
+            else:
+                b = blocks(self.refs, g, what, cc)
             return rcopy(b, b, ss, rs, me.sibling())
         way, k = (i - 10) // 3, (i - 10) % 3 + 1
         b = blocks(self.refs, g, ways[way][side], c, lax.rem(me.z + 4 - k, 4))
@@ -369,13 +374,17 @@
             self.copy(g, i, True).wait_recv()
 
     def start(self, g):
-        self.go(g, 0, 1, 3, 4, 5)
+        self.go(g, *((0, 1) if g == PLANE else (0, 1, 3, 4, 5)))
 
     def step0(self, g):
         self.got(g, 0)
         self.go(g, 2)
 
     def step1(self, g):
+        if g == PLANE:
+            self.got(g, 1, 2)
+            self.go(g, 3, 4, 5, 6)
+            return
         for k in range(3):
             self.got(g, 3 + k)
             self.go(g, 13 + k, 10 + k)
@@ -392,6 +401,11 @@
         self.go(g, 8)
 
     def step4(self, g):
+        if g == PLANE:
+            for i in (3, 4, 5):
+                self.got(g, i)
+                self.go(g, i + 4)
+            return
         self.got(g, 2, 16, 17, 18)
         self.go(g, 9)
 
@@ -399,7 +413,7 @@
         self.got(g, 6, 7, 8, 9)
 
     def sent(self, g):
-        for i in range(19):
+        for i in range(10 if g == PLANE else 19):
             self.copy(g, i).wait_send()
 
 
@@ -724,11 +738,12 @@
             r.first[rows, lanes] = out.astype(BF)
 
 
-def level_two(r):
+def level_two(r, hooks=None):
     r.q2[...] = dg(r.first[...], weight(r, 5), 1, 1).astype(BF)
 
     @pl.loop(0, HEADS // 2)
     def _(p):
+        at_steps(p, hooks)
         lanes = pair_lanes(p)
         _, scores = scores_of(r.q2[:, lanes], r.kp[0, :, lanes])
         out = softmax_out(scores, r.bias2[...], r.kp[1, :, lanes], r.lse, p + HEADS // 2)
@@ -761,27 +776,28 @@
         r.hlow[rows] = (n * r.gains[0:1] + r.shifts[0:1]).astype(BF)
 
 
-def ffn_up(r):
+def ffn_up(r, hooks=None):
     k = math.sqrt(2.0 / math.pi)
 
     @pl.loop(0, 4)
     def _(j):
+        at_steps(j, hooks)
         for i in range(2):
             rows = pl.ds(256 * i, 256)
             u = dg(r.hlow[rows], weight_up(r, j), 1, 0)
             square = u * u
-            t = jnp.tanh(k * u * (1.0 + 0.044715 * square))
-            half = 0.5 * (1.0 + t)
-            r.act[j, rows] = (u * half).astype(BF)
-            slope = half + (0.5 * k) * u * (1.0 - t * t) * (1.0 + (3 * 0.044715) * square)
+            half = 0.5 + 0.5 * jnp.tanh(u * (k + (k * 0.044715) * square))
+            value = u * half
+            r.act[j, rows] = value.astype(BF)
+            slope = half + value * (1.0 - half) * (2 * k + (6 * k * 0.044715) * square)
             r.gd[j, rows] = slope.astype(BF)
 
 
-def ffn_down(r, lo, hi):
+def ffn_down(r, lo, hi, first):
     @pl.loop(0, 2)
     def _(i):
         rows = pl.ds(pl.multiple_of(256 * i, 256), 256)
-        total = r.acc[rows] if lo else None
+        total = None if first else r.acc[rows]
         for j in range(4):
             term = dg(r.act[j, rows, lo:hi], weight_down(r, j // 2, j % 2, lo, hi), 1, 1)
             total = term if total is None else total + term
@@ -811,12 +827,11 @@
         j = y * 2 + c
         t = dg(r.dlow[...], weight_down(r, y, c, lo, hi), 1, 0)
         r.gd[j, :, lo:hi] = (r.gd[j, :, lo:hi].astype(F32) * t).astype(BF)
-        for i in range(2):
-            g = dg(r.dlow[:, 384 * i : 384 * i + 384], r.act[j, :, lo:hi], 0, 0).astype(BF)
-            r.down[2 * i : 2 * i + 2, :, y, c, :, lo:hi] = g.reshape(2, 2, 96, hi - lo)
-
-
-def back_first_norm(r):
+        g = dg(r.dlow[...], r.act[j, :, lo:hi], 0, 0).astype(BF)
+        r.down[:, :, y, c, :, lo:hi] = g.reshape(4, 2, 96, hi - lo)
+
+
+def back_hidden(r):
     @pl.loop(0, 2)
     def _(i):
         rows = pl.ds(pl.multiple_of(256 * i, 256), 256)
@@ -825,6 +840,8 @@
             total = total + dg(r.gd[j, rows], weight_up(r, j), 1, 1)
         r.acc[rows] = total
 
+
+def back_first_norm(r):
     @pl.loop(0, 4)
     def _(i):
         rows = pl.ds(pl.multiple_of(i * 128, 128), 128)
@@ -995,7 +1012,7 @@
     vbuf=((10, 16, 768), F32),
     **ACTIVE,
 )
-SEMS = dict(load=20, swap=2, ag_s=(N_GROUPS, 19), ag_r=(N_GROUPS, 19), rs_s=(N_GROUPS, 10), rs_r=(N_GROUPS, 10), vs=7, vr=7, ends=4, endr=4, outs=13)
+SEMS = dict(load=20, swap=2, ag_s=(N_GROUPS, 19), ag_r=(N_GROUPS, 19), rs_s=(N_GROUPS, 10), rs_r=(N_GROUPS, 10), vs=7, vr=7, ends=N_GROUPS, endr=N_GROUPS, outs=2 * N_GROUPS)
 
 
 def layer_kernel(*refs):
@@ -1042,29 +1059,34 @@
     )
 
     loads[7].wait()
-    gat.start(6)
+    gat.start(8)
+    gat.go(6, 0, 1)
     for cp in loads[:7]:
         cp.wait()
     place_squares(me, shards, r.sq, r.act, r.swap.at[0], r.swap.at[1])
-    for g in range(4):
+    for g in (0, 1, 9, 2, 3):
         gat.start(g)
+    gat.step0(8)
     gat.step0(6)
     loads[8].wait()
-    for g in (4, 5, 7, 8):
-        gat.start(g)
+    gat.start(4)
+    gat.start(5)
+    gat.go(6, 3, 4, 5)
+    gat.start(7)
     set_masks(r, r.length[0])
-    gat.step1(6)
     gat.step0(0)
     gat.step0(1)
     gat.step1(0)
+    gat.step0(9)
     gat.step0(2)
     gat.step1(1)
+    gat.step1(9)
     gat.step0(3)
-    gat.step2(6)
     gat.step2(0)
     gat.step1(2)
     gat.step0(4)
     gat.step2(1)
+    gat.step2(9)
     gat.step3(0)
     gat.step1(3)
     gat.step0(5)
@@ -1077,49 +1099,52 @@
     gat.arrived(0)
     project(r, 0, 1)
     gat.step2(3)
+    gat.step3(9)
     gat.step3(2)
     gat.step4(1)
     gat.step1(5)
     gat.step0(7)
-    gat.step0(8)
+    gat.step4(9)
+    gat.arrived(1)
+    project(r, 1, 2)
+    gat.step1(6)
+    gat.step2(4)
+    gat.arrived(9)
+    project(r, 2, 3)
     gat.step1(7)
-    gat.arrived(1)
-    project(r, 1, 3)
-    gat.step2(4)
-    gat.step3(3)
-    gat.step4(2)
     gat.step1(8)
+
+    def ahead_a():
+        gat.step4(2)
+        gat.step2(5)
+
+    level_one(r, {2: lambda: gat.step3(3), 4: ahead_a})
+    gat.step3(4)
     gat.arrived(2)
     project_pool(r, 0)
     project_pool(r, 1)
-
-    def ahead_b():
-        gat.step3(4)
-        gat.step4(3)
-
-    level_one(r, {2: lambda: gat.step2(5), 4: ahead_b})
-    gat.step2(7)
-    gat.step3(5)
-    gat.step3(6)
-    gat.step4(6)
-    gat.step4(4)
+    gat.step4(3)
+    gat.step2(6)
     gat.arrived(3)
-    level_two(r)
-    gat.step2(8)
-    gat.step3(7)
+
+    def ahead_c():
+        gat.step4(4)
+        gat.step3(5)
+
+    level_two(r, {3: ahead_c, 5: lambda: gat.step2(7)})
+    first_norm(r)
     gat.step4(5)
-    first_norm(r)
-    gat.step3(8)
-    gat.step4(7)
     gat.arrived(4)
     gat.arrived(5)
-    ffn_up(r)
-    gat.step4(8)
+    ffn_up(r, {1: lambda: gat.step3(6), 2: lambda: gat.step4(8), 3: lambda: gat.step4(6)})
+    gat.step3(7)
+    gat.arrived(8)
+    ffn_down(r, 512, 768, True)
     gat.arrived(6)
+    gat.step4(7)
+    ffn_down(r, 0, 256, False)
     gat.arrived(7)
-    ffn_down(r, 0, 512)
-    gat.arrived(8)
-    ffn_down(r, 512, 768)
+    ffn_down(r, 256, 512, False)
     second_norm(r)
     out = pltpu.make_async_copy(r.og, r.out, r.load.at[0])
     out.start()
@@ -1165,10 +1190,11 @@
         back_down(r, me.c, lo, hi)
         sca.step1(g)
     sca.step2(6)
-    back_first_norm(r)
+    back_hidden(r)
     grad_up(r)
     sca.start(4)
     sca.start(5)
+    back_first_norm(r)
     sca.step2(7)
     sca.step3(6)
     back_out(r)
@@ -1188,22 +1214,24 @@
     back_level_one(
         r,
         {
+            0: lambda: sca.step2(4),
             2: lambda: sca.step1(2),
-            3: lambda: sca.step2(4),
+            5: lambda: sca.step2(5),
             7: total.send_core,
-            8: lambda: sca.step2(5),
             9: total.send_beside,
             11: lambda: sca.step3(4),
         },
     )
     finish_projection(r, 1, r.dqkv[1])
+    sca.start(1)
     finish_projection(r, 2, r.dqkv[2])
-    sca.start(1)
+    sca.start(9)
+    sca.step1(1)
     sca.step2(3)
-    sca.step3(5)
     finish_projection(r, 0, r.dqkv[0])
     sca.start(0)
-    sca.step1(1)
+    sca.step1(9)
+    sca.step3(5)
     sca.step1(0)
     sca.step3(8)
     r.dlow[...] = r.dr[...].astype(BF)
@@ -1213,12 +1241,14 @@
     sca.step3(3)
     for g in (6, 7, 4, 5):
         give(g)
+    sca.step2(1)
     sca.step3(2)
-    sca.step2(1)
+    sca.step2(9)
+    give(8)
+    sca.step3(1)
     sca.step2(0)
-    give(8)
     end(3)
-    sca.step3(1)
+    sca.step3(9)
     sca.step3(0)
     end(2)
     close(3)
@@ -1227,12 +1257,14 @@
     vec_out = pltpu.make_async_copy(r.vec, r.o_vec, r.load.at[2])
     vec_out.start()
     end(1)
+    end(9)
     end(0)
     for g in range(N_GROUPS):
         sca.sent(g)
     close(1)
+    close(9)
     close(0)
-    for g in range(4):
+    for g in SQUARES:
         end_swap(g).wait_send()
     for cp in [*pending, out, din, vec_out]:
         cp.wait()

time: 186 us -> 177 us (0.952)
  Pallas kernels: 185 us -> 175 us
    pallas_call x1, Pallas kernels: 181 us -> 172 us  [layer(): pl.pallas_call(layer_kernel, out_shape=[jax.ShapeDtypeStruct((512, 768),...]
where the time goes in v4:
time: 177 us
  Pallas kernels  175 us (99%)
    pallas_call x1, Pallas kernels, layer(): pl.pallas_call(layer_kernel, out_shape=[jax.ShapeDtypeStruct((512, 768),...  172 us

profile of v4, /device:TPU:1, one launch (start us, length us, event | category | flops | bytes accessed | tf_op | source)
XLA Modules:
  0.0 176.7 jit_solution(6681081952820766478)
XLA Ops:
  1.3 171.7 %shard_map.254 = (bf16[512,768]{1,0:T(8,128)(2,1)}, bf16[512,768]{1,0:T(8,128)(2,1)}, f32[16,768]{1,0:T(8,128)}, f32[7,2,48,384]{3,2,1,0:T(8,128)}, f32[192,384]{1,0:T(8,128)}, /*index=5*/f32[96,768]{1,0:T(8,128)}) custom-call(s32[1]{0:T(128)S(6)} %copy.29.refs_0_, bf16[512,768]{1,0:T(8,128)(2,1)} %refs_1_.1, bf16[512,768]{1,0:T(8,128)(2,1)} %refs_2_.1, ...), custom_call_target="tpu_custom_call" | custom-call | tf_op jit(solution)/shard_map/pallas_call | solution.py:1275
  173.0 3.5 %shard_map.255 = (bf16[512,768]{1,0:T(8,128)(2,1)}, bf16[512,768]{1,0:T(8,128)(2,1)}, f32[192,96]{1,0:T(8,128)}, f32[192,96]{1,0:T(8,128)}, f32[192,96]{1,0:T(8,...) custom-call(bf16[512,768]{1,0:T(8,128)(2,1)} %get-tuple-element.34.r, ...), custom_call_target="tpu_custom_call" | custom-call | tf_op jit(solution)/shard_map/pallas_call | solution.py:1327

commit v5 on v4

--- a/solution.py
+++ b/solution.py
@@ -324,6 +324,16 @@
     return down.at[z, x, y, c, :, lo:hi]
 
 
+def half(refs, g, c):
+    sq, up, down = refs
+    kind, lo, hi = GROUPS[g]
+    if kind == "s":
+        return sq.at[lo:hi, :, :, c]
+    if kind == "u":
+        return up.at[:, c, :, :, lo:hi]
+    return down.at[:, :, :, c, :, lo:hi]
+
+
 def plane(down, g, c, z):
     _, lo, hi = GROUPS[g]
     return down.at[z, :, :, c, :, lo:hi]
@@ -341,7 +351,10 @@
 
     def copy(self, g, i, incoming=False):
         me = self.me
-        ss, rs = self.ssem.at[g, i], self.rsem.at[g, i]
+        together = min(i, 6) if i < 10 else (i - 10) // 3
+        first = 0 if i in (3, 4, 5) and g != PLANE else together
+        ss = self.ssem.at[g, i - 7 if i in (10, 11, 12) else first]
+        rs = self.rsem.at[g, i - 3 if i in (10, 11, 12) else together]
         side = 1 if incoming else 0
         c = me.c
         ways = ((me.own, me.p1), (me.own, me.p2), (me.p1, me.diag))
@@ -373,6 +386,9 @@
         for i in which:
             self.copy(g, i, True).wait_recv()
 
+    def whole(self, g, at, ref):
+        return rcopy(ref, ref, self.ssem.at[g, at], self.rsem.at[g, at], self.me.sibling())
+
     def start(self, g):
         self.go(g, *((0, 1) if g == PLANE else (0, 1, 3, 4, 5)))
 
@@ -397,7 +413,7 @@
         self.go(g, 7)
 
     def step3(self, g):
-        self.got(g, 1, 13, 14, 15)
+        self.whole(g, 1, blocks(self.refs, g, self.me.p2, self.me.c)).wait_recv()
         self.go(g, 8)
 
     def step4(self, g):
@@ -406,15 +422,23 @@
                 self.got(g, i)
                 self.go(g, i + 4)
             return
-        self.got(g, 2, 16, 17, 18)
+        self.whole(g, 2, blocks(self.refs, g, self.me.diag, self.me.c)).wait_recv()
         self.go(g, 9)
 
     def arrived(self, g):
-        self.got(g, 6, 7, 8, 9)
+        self.whole(g, 6, half(self.refs, g, 1 - self.me.c)).wait_recv()
 
     def sent(self, g):
-        for i in range(10 if g == PLANE else 19):
-            self.copy(g, i).wait_send()
+        me = self.me
+        if g == PLANE:
+            for i in range(6):
+                self.copy(g, i).wait_send()
+        else:
+            for at in range(3):
+                self.whole(g, at, blocks(self.refs, g, me.own, me.c)).wait_send()
+            for i in (10, 11, 12):
+                self.copy(g, i).wait_send()
+        self.whole(g, 6, half(self.refs, g, me.c)).wait_send()
 
 
 class Scatter:
@@ -453,7 +477,7 @@
     def copy(self, g, i):
         me = self.me
         c = me.c
-        ss, rs = self.ssem.at[g, i], self.rsem.at[g, i]
+        ss, rs = self.ssem.at[g, max(i - 3, 0)], self.rsem.at[g, i]
         if g == PLANE:
             if i < 4:
                 z = me.peer(i + 1)
@@ -550,7 +574,9 @@
         return total
 
     def sent(self, g):
-        for i in range(10):
+        away = half(self.refs, g, 1 - self.me.c)
+        rcopy(away, away, self.ssem.at[g, 0], self.rsem.at[g, 0], self.me.sibling()).wait_send()
+        for i in range(4, 10):
             self.copy(g, i).wait_send()
 
 
@@ -1012,7 +1038,9 @@
     vbuf=((10, 16, 768), F32),
     **ACTIVE,
 )
-SEMS = dict(load=20, swap=2, ag_s=(N_GROUPS, 19), ag_r=(N_GROUPS, 19), rs_s=(N_GROUPS, 10), rs_r=(N_GROUPS, 10), vs=7, vr=7, ends=N_GROUPS, endr=N_GROUPS, outs=2 * N_GROUPS)
+SEMS = dict(
+    load=18, swap=2, send=(N_GROUPS, 7), ag_r=(N_GROUPS, 10), rs_r=(N_GROUPS, 10), vs=7, vr=7, ends=5, endr=5
+)
 
 
 def layer_kernel(*refs):
@@ -1045,7 +1073,7 @@
         cp.start()
     greet(me)
     weights = (r.sq, r.up, r.down)
-    gat = Gather(me, weights, r.ag_s, r.ag_r)
+    gat = Gather(me, weights, r.send, r.ag_r)
     sca = Scatter(
         me,
         weights,
@@ -1054,7 +1082,7 @@
         (r.r2_sq, r.r2_up, r.r2_down),
         (r.r3_sq, r.r3_up, r.r3_down),
         (r.pz, r.p2, r.p1),
-        r.rs_s,
+        r.send,
         r.rs_r,
     )
 
@@ -1151,8 +1179,8 @@
     for g in range(N_GROUPS):
         gat.sent(g)
 
-    def flush(src, dst, i):
-        cp = pltpu.make_async_copy(src, dst, r.outs.at[i])
+    def flush(src, dst):
+        cp = pltpu.make_async_copy(src, dst, r.load.at[3 + len(pending)])
         cp.start()
         pending.append(cp)
 
@@ -1162,26 +1190,27 @@
         kind, lo, hi = GROUPS[g]
         if kind == "u":
             r.b_up[lo:hi] = sca.finish(g)
-            flush(r.b_up.at[lo:hi], r.o_up.at[lo:hi], g)
+            flush(r.b_up.at[lo:hi], r.o_up.at[lo:hi])
         else:
             r.b_down[:, lo:hi] = sca.finish(g)
-            flush(r.b_down.at[:, lo:hi], r.o_down.at[:, lo:hi], g)
+            flush(r.b_down.at[:, lo:hi], r.o_down.at[:, lo:hi])
 
     def end_swap(g, incoming=False):
         _, lo, hi = GROUPS[g]
         b = r.b_sq.at[lo:hi, 1 - me.c if incoming else me.c]
-        return rcopy(b, b, r.ends.at[g], r.endr.at[g], me.sibling())
+        at = SQUARES.index(g)
+        return rcopy(b, b, r.ends.at[at], r.endr.at[at], me.sibling())
 
     def end(g):
         _, lo, hi = GROUPS[g]
         r.b_sq[lo:hi, me.c] = sca.finish(g)
         end_swap(g).start()
-        flush(r.b_sq.at[lo:hi, me.c], r.o_sq.at[lo:hi, me.c], g)
+        flush(r.b_sq.at[lo:hi, me.c], r.o_sq.at[lo:hi, me.c])
 
     def close(g):
         _, lo, hi = GROUPS[g]
         end_swap(g, True).wait_recv()
-        flush(r.b_sq.at[lo:hi, 1 - me.c], r.o_sq.at[lo:hi, 1 - me.c], N_GROUPS + g)
+        flush(r.b_sq.at[lo:hi, 1 - me.c], r.o_sq.at[lo:hi, 1 - me.c])
 
     for g in (6, 8, 7):
         _, lo, hi = GROUPS[g]

time: 177 us -> 173 us (0.977)
  Pallas kernels: 175 us -> 172 us
    pallas_call x1, Pallas kernels: 172 us -> 168 us  [layer(): pl.pallas_call(layer_kernel, out_shape=[jax.ShapeDtypeStruct((512, 768),...]
where the time goes in v5:
time: 173 us
  Pallas kernels  172 us (99%)
    pallas_call x1, Pallas kernels, layer(): pl.pallas_call(layer_kernel, out_shape=[jax.ShapeDtypeStruct((512, 768),...  168 us
    pallas_call x1, Pallas kernels, ending(): pl.pallas_call(ending_kernel, out_shape=[jax.ShapeDtypeStruct(*s) for s i...  3.5 us

profile of v5, /device:TPU:1, one launch (start us, length us, event | category | flops | bytes accessed | tf_op | source)
XLA Modules:
  0.0 173.3 jit_solution(14753230803248525842)
XLA Ops:
  1.3 168.3 %shard_map.254 = (bf16[512,768]{1,0:T(8,128)(2,1)}, bf16[512,768]{1,0:T(8,128)(2,1)}, f32[16,768]{1,0:T(8,128)}, f32[7,2,48,384]{3,2,1,0:T(8,128)}, f32[192,384]{1,0:T(8,128)}, /*index=5*/f32[96,768]{1,0:T(8,128)}) custom-call(s32[1]{0:T(128)S(6)} %copy.29.refs_0_, bf16[512,768]{1,0:T(8,128)(2,1)} %refs_1_.1, bf16[512,768]{1,0:T(8,128)(2,1)} %refs_2_.1, ...), custom_call_target="tpu_custom_call" | custom-call | tf_op jit(solution)/shard_map/pallas_call | solution.py:1304
  169.6 3.5 %shard_map.255 = (bf16[512,768]{1,0:T(8,128)(2,1)}, bf16[512,768]{1,0:T(8,128)(2,1)}, f32[192,96]{1,0:T(8,128)}, f32[192,96]{1,0:T(8,128)}, f32[192,96]{1,0:T(8,...) custom-call(bf16[512,768]{1,0:T(8,128)(2,1)} %get-tuple-element.34.r, ...), custom_call_target="tpu_custom_call" | custom-call | tf_op jit(solution)/shard_map/pallas_call | solution.py:1356

commit v6 on v5

--- a/solution.py
+++ b/solution.py
@@ -1160,8 +1160,8 @@
         gat.step3(5)
 
     level_two(r, {3: ahead_c, 5: lambda: gat.step2(7)})
+    gat.step4(5)
     first_norm(r)
-    gat.step4(5)
     gat.arrived(4)
     gat.arrived(5)
     ffn_up(r, {1: lambda: gat.step3(6), 2: lambda: gat.step4(8), 3: lambda: gat.step4(6)})

time: 173 us -> 174 us (level)
  no operation moved by 1% of the time
where the time goes in v6:
time: 174 us
  Pallas kernels  172 us (99%)
    pallas_call x1, Pallas kernels, layer(): pl.pallas_call(layer_kernel, out_shape=[jax.ShapeDtypeStruct((512, 768),...  169 us
    pallas_call x1, Pallas kernels, ending(): pl.pallas_call(ending_kernel, out_shape=[jax.ShapeDtypeStruct(*s) for s i...  3.5 us

profile of v6, /device:TPU:1, one launch (start us, length us, event | category | flops | bytes accessed | tf_op | source)
XLA Modules:
  0.0 173.8 jit_solution(1489203972445092487)
XLA Ops:
  1.3 168.8 %shard_map.254 = (bf16[512,768]{1,0:T(8,128)(2,1)}, bf16[512,768]{1,0:T(8,128)(2,1)}, f32[16,768]{1,0:T(8,128)}, f32[7,2,48,384]{3,2,1,0:T(8,128)}, f32[192,384]{1,0:T(8,128)}, /*index=5*/f32[96,768]{1,0:T(8,128)}) custom-call(s32[1]{0:T(128)S(6)} %copy.29.refs_0_, bf16[512,768]{1,0:T(8,128)(2,1)} %refs_1_.1, bf16[512,768]{1,0:T(8,128)(2,1)} %refs_2_.1, ...), custom_call_target="tpu_custom_call" | custom-call | tf_op jit(solution)/shard_map/pallas_call | solution.py:1304
  170.1 3.5 %shard_map.255 = (bf16[512,768]{1,0:T(8,128)(2,1)}, bf16[512,768]{1,0:T(8,128)(2,1)}, f32[192,96]{1,0:T(8,128)}, f32[192,96]{1,0:T(8,128)}, f32[192,96]{1,0:T(8,...) custom-call(bf16[512,768]{1,0:T(8,128)(2,1)} %get-tuple-element.34.r, ...), custom_call_target="tpu_custom_call" | custom-call | tf_op jit(solution)/shard_map/pallas_call | solution.py:1356
